TPU v7x, 128 devices: a whole 4x4x4 slice. The times are simulated.
128 devices in a mesh: branch: 2 (over x_lo), seq: 16 (over x_hi, z, core), tp: 4 (over y).
Axes of the slice: x: 4 (x_hi: 2, x_lo: 2; x = x_hi * 2 + x_lo), y: 4, z: 4, core: 2. Of those that a mesh axis runs over, the one named last changes fastest.
Arguments:
- hidden: bfloat16 [2, 8192, 4096], P('branch', 'seq', 'tp'), may hold values from -6 to 6
- modulation: float32 [2, 4, 4096], P('branch'), may hold values from -4 to 4
- qkv_weight: bfloat16 [2, 4096, 3, 2048], P('branch', None, None, 'tp'), as said below
- out_weight: bfloat16 [2, 2048, 4096], P('branch', 'tp'), may hold values from -0.5 to 0.5
- control_proj: bfloat16 [4096, 4096], P('tp'), may hold values from -0.09375 to 0.09375
- cached_mlp: bfloat16 [2, 8192, 4096], P('branch', 'seq', 'tp'), may hold values from -6 to 6
Outputs:
- updated: bfloat16 [2, 8192, 4096], P('branch', 'seq', 'tp')
Inputs may be any that keep to these rules, and one draw needn't show every extreme that they name: `qkv_weight`: entries are of order 4096^-1/2 times a factor.
All inputs are finite; a program needn't handle non-finite values.
Results may differ from a plain program's by a relative error of at most 0.02.
Values may be sent and summed in bfloat16 or wider, within the bound.
No kernel may reach another device: no remote copies, remote signals or barrier semaphores. Data moves between devices by JAX's collectives and lax.ppermute only.
A program may use at most 256 MiB of HBM per device.

v0:
```python
import jax
import jax.numpy as jnp
from jax import lax
from jax.sharding import PartitionSpec as P

HEAD_DIM = 128


def passed_along(value, axis, by):
    size = lax.axis_size(axis)
    pairs = [(i, i + by) for i in range(size) if 0 <= i + by < size]
    return lax.ppermute(value, axis, pairs)


def body(hidden, modulation, qkv_weight, out_weight, control_proj, cached_mlp):
    shard_rows = hidden[0]
    row_total = shard_rows.shape[0]
    width_here = shard_rows.shape[1]
    whole_rows = lax.all_gather(shard_rows, "tp", axis=1, tiled=True)
    modulation_rows = modulation[0]
    widened = whole_rows.astype(jnp.float32)
    row_mean = jnp.mean(widened, axis=-1, keepdims=True)
    centred = widened - row_mean
    row_var = jnp.mean(centred * centred, axis=-1, keepdims=True)
    normed = centred * lax.rsqrt(row_var + 1e-06)
    modulated = (normed * (1.0 + modulation_rows[1]) + modulation_rows[0]).astype(jnp.bfloat16)
    projected = jnp.einsum(
        "td,dcw->ctw", modulated, qkv_weight[0], preferred_element_type=jnp.float32
    )
    projected = projected.astype(jnp.bfloat16)
    heads_here = projected.shape[2] // HEAD_DIM
    query = projected[0].reshape(row_total, heads_here, HEAD_DIM)
    score_scale = 1.0 / HEAD_DIM**0.5
    running_max = jnp.full((heads_here, row_total), -1e30, jnp.float32)
    key_rows = lax.all_gather(projected[1], "seq", axis=0, tiled=True)
    value_rows = lax.all_gather(projected[2], "seq", axis=0, tiled=True)
    row_count = key_rows.shape[0]
    key_rows = key_rows.reshape(row_count, heads_here, HEAD_DIM)
    value_rows = value_rows.reshape(row_count, heads_here, HEAD_DIM)
    scores = (
        jnp.einsum("thd,nhd->htn", query, key_rows, preferred_element_type=jnp.float32)
        * score_scale
    )
    new_max = jnp.maximum(running_max, jnp.max(scores, axis=-1))
    weights = jnp.exp(scores - new_max[..., None])
    running_sum = jnp.sum(weights, axis=-1)
    update = jnp.einsum(
        "htn,nhd->htd", weights.astype(jnp.bfloat16), value_rows, preferred_element_type=jnp.float32
    )
    weighted = update
    running_max, running_sum, weighted = (new_max, running_sum, weighted)
    attended = (
        (weighted / running_sum[..., None])
        .transpose(1, 0, 2)
        .reshape(row_total, heads_here * HEAD_DIM)
    )
    attended = attended.astype(jnp.bfloat16)
    partial_value = jnp.dot(attended, out_weight[0], preferred_element_type=jnp.float32)
    first_column = lax.axis_index("tp") * width_here
    gate_slice = lax.dynamic_slice_in_dim(modulation_rows, first_column, width_here, 1)
    section = lax.axis_index("branch")
    empty_terms = jnp.zeros((row_total, control_proj.shape[1]), jnp.float32)
    cache_term = gate_slice[3] * cached_mlp[0].astype(jnp.float32)
    attention = lax.psum_scatter(
        partial_value.astype(jnp.bfloat16), "tp", scatter_dimension=1, tiled=True
    ).astype(jnp.float32)
    blended = shard_rows.astype(jnp.float32) + gate_slice[2] * attention + cache_term
    rounded = blended.astype(jnp.bfloat16)
    terms = lax.cond(
        section == 0,
        lambda: jnp.dot(rounded, control_proj, preferred_element_type=jnp.float32),
        lambda: empty_terms,
    )
    summed = lax.psum_scatter(
        terms.astype(jnp.bfloat16), "tp", scatter_dimension=1, tiled=True
    ).astype(jnp.float32)
    joined = passed_along(summed.astype(jnp.bfloat16), "branch", 1).astype(summed.dtype)
    return (blended + joined).astype(jnp.bfloat16)[None]


def solution(mesh):
    placed = (
        P("branch", "seq", "tp"),
        P("branch", None, None),
        P("branch", None, None, "tp"),
        P("branch", "tp", None),
        P("tp", None),
        P("branch", "seq", "tp"),
    )
    return jax.shard_map(
        body, mesh=mesh, in_specs=placed, out_specs=P("branch", "seq", "tp"), check_vma=False
    )
```

profile of v0, /device:TPU:2, one launch (start us, length us, event | category | flops | bytes accessed | tf_op | source)
XLA Modules:
  0.0 404.9 jit_solution(7916484718593898387)
XLA Ops:
  6.5 0.0 all-gather.7.cloned.1.call-start
  6.5 0.7 all-gather.7.cloned.1.call-update
  7.3 0.0 all-gather.9.cloned.1.call-start
  7.3 1.0 slice_add_fusion
  8.3 51.4 %all-gather.7.cloned.1.call-done = bf16[1,512,4096]{2,1,0:T(8,128)(2,1)} async-done(((bf16[1,512,1024]{2,1,0:T(8,128)(2,1)}), bf16[1,512,4096]{2,1,0:T(8,128)(2,1)}) %all-gather.7.cloned.1.call-update) | async-done | bytes 4194320 | tf_op jit(solution)/shard_map/all_gather | solution.py:19
  59.7 0.0 copy-start
  59.7 3.0 convert_reduce_fusion
  62.7 3.4 fusion.9
  66.1 0.0 copy-done
  66.1 10.1 %fusion.26 = bf16[3,512,512]{1,2,0:T(8,128)(2,1)S(1)} fusion(bf16[1,4096,3,512]{3,1,2,0:T(8,128)(2,1)} %param.10, bf16[1,512,4096]{2,1,0:T(8,128)(2,1)S(1)} %copy-done, f32[4096]{0:T(1024)S(1)} %bitcast.83, f32[4096]{0:T(1024)S(1)} %bitcast.82, f32[512]{0:T(512)S(1)} %add_rsqrt_fusion, f32[512]{0:T(512)S(1)} %broadcast_multiply_fusion), kind=kOutput, calls=%fused_computation.28 | convolution fusion | flops 6455820288 | bytes 18386944 | tf_op jit(solution)/shard_map/td,dcw->ctw/dot_general | solution.py:27
  76.2 1.1 fusion.43
  77.3 0.0 all-gather.9.cloned.1.call-update
  77.4 0.0 all-gather.11.cloned.1.call-start
  77.4 0.7 all-gather.11.cloned.1.call-update
  78.1 0.2 reduce-scatter.3.cloned.1.call-start
  78.3 75.9 %all-gather.9.cloned.1.call-done = bf16[1,8192,512]{1,2,0:T(8,128)(2,1)} async-done(((bf16[1,512,512]{1,2,0:T(8,128)(2,1)}), bf16[1,8192,512]{1,2,0:T(8,128)(2,1)}) %all-gather.9.cloned.1.call-update) | async-done | bytes 8388624 | tf_op jit(solution)/shard_map/all_gather | solution.py:35
  154.2 27.2 %multiply_reduce_fusion = (f32[4,512]{1,0:T(4,128)S(1)}, f32[4,512,8192]{2,1,0:T(8,128)}) fusion(bf16[512,4,128]{0,2,1:T(8,128)(2,1)S(1)} %bitcast.76, bf16[8192,4,128]{0,2,1:T(8,128)(2,1)} %bitcast.73), kind=kOutput, calls=%fused_computation.1 | convolution fusion | flops 4328519680 | bytes 76029952 | tf_op jit(solution)/shard_map/thd,nhd->htn/dot_general | solution.py:41
  181.4 22.3 %fusion = f32[4,512]{1,0:T(4,128)S(1)} fusion(f32[4,512,8192]{2,1,0:T(8,128)} %get-tuple-element.24, f32[4,512]{1,0:T(4,128)S(1)} %broadcast_maximum_fusion), kind=kLoop, calls=%fused_computation.2 | loop fusion | flops 50329600 | bytes 67125248 | tf_op jit(solution)/shard_map/reduce_sum | solution.py:46
  203.7 27.5 %all-gather.11.cloned.1.call-done = bf16[1,8192,512]{1,2,0:T(8,128)(2,1)} async-done(((bf16[1,512,512]{1,2,0:T(8,128)(2,1)}), bf16[1,8192,512]{1,2,0:T(8,128)(2,1)}) %all-gather.11.cloned.1.call-update) | async-done | bytes 8388624 | tf_op jit(solution)/shard_map/all_gather | solution.py:36
  231.2 26.3 %fusion.37 = bf16[512,4,128]{0,2,1:T(8,128)(2,1)S(1)} fusion(bf16[8192,4,128]{0,2,1:T(8,128)(2,1)} %bitcast.74, f32[4,512,8192]{2,1,0:T(8,128)} %get-tuple-element.24, f32[4,512]{1,0:T(4,128)S(1)} %broadcast_maximum_fusion, f32[512,4]{0,1:T(4,128)S(1)} %bitcast.77), kind=kOutput, calls=%fused_computation.31 | convolution fusion | flops 4345823232 | bytes 76038144 | tf_op jit(solution)/shard_map/htn,nhd->htd/dot_general | solution.py:47
  257.5 0.0 copy-start.1
  257.5 0.0 copy-start.2
  257.5 6.6 %convolution_convert_fusion = bf16[512,4096]{1,0:T(8,128)(2,1)} fusion(bf16[512,512]{0,1:T(8,128)(2,1)S(1)} %bitcast.75, bf16[1,512,4096]{2,1,0:T(8,128)(2,1)} %param.11), kind=kOutput, calls=%fused_computation.16 | convolution fusion | flops 2149580800 | bytes 8912896 | tf_op jit(solution)/shard_map/dot_general | solution.py:58
  264.2 0.0 reduce-scatter.3.cloned.1.call-update
  264.2 0.0 reduce-scatter.5.cloned.1.call-start
  264.3 0.9 constant_dynamic-slice_fusion
  265.2 44.4 %reduce-scatter.3.cloned.1.call-done = bf16[512,1024]{1,0:T(8,128)(2,1)} async-done(((bf16[512,4096]{1,0:T(8,128)(2,1)}), bf16[512,1024]{1,0:T(8,128)(2,1)}) %reduce-scatter.3.cloned.1.call-update) | async-done | bytes 1048592 | tf_op jit(solution)/shard_map/reduce_scatter | solution.py:64
  309.6 0.0 copy-done.1
  309.6 0.0 copy-done.2
  309.6 2.9 fusion.40
  312.4 0.0 copy-start.3
  312.4 2.4 conditional.1
  312.4 2.4 broadcast_in_dim.0
  314.9 0.0 reduce-scatter.5.cloned.1.call-update
  314.9 54.5 %reduce-scatter.5.cloned.1.call-done = bf16[512,1024]{1,0:T(8,128)(2,1)} async-done(((bf16[512,4096]{1,0:T(8,128)(2,1)}), bf16[512,1024]{1,0:T(8,128)(2,1)}) %reduce-scatter.5.cloned.1.call-update) | async-done | bytes 1048592 | tf_op jit(solution)/shard_map/reduce_scatter | solution.py:74
  369.4 1.3 collective-permute-start
  370.7 25.8 %collective-permute-done = bf16[512,1024]{1,0:T(8,128)(2,1)S(1)} collective-permute-done((bf16[512,1024]{1,0:T(8,128)(2,1)}, bf16[512,1024]{1,0:T(8,128)(2,1)S(1)}, u32[]{:S(2)}, u32[]{:S(2)}) %collective-permute-start) | collective-permute-done | bytes 1048608 | tf_op jit(solution)/shard_map/ppermute | solution.py:12
  396.4 0.0 copy-done.3
  396.4 1.9 fusion.41
  (3 shorter events, 0.0 us)
Async XLA Ops:
  6.5 53.2 %all-gather.7.cloned.1.call-start = ((), (), s32[]{:S(2)}) async-start(), calls=%async_computation.4 | async-start | bytes 5242880 | tf_op jit(solution)/shard_map/all_gather | solution.py:19
  7.3 146.9 %all-gather.9.cloned.1.call-start = ((), (), s32[]{:S(2)}) async-start(), calls=%async_computation.5 | async-start | bytes 8912896 | tf_op jit(solution)/shard_map/all_gather | solution.py:35
  59.7 6.4 %copy-start = (bf16[1,512,4096]{2,1,0:T(8,128)(2,1)S(1)}, bf16[1,512,4096]{2,1,0:T(8,128)(2,1)}, u32[]{:S(2)}) copy-start(bf16[1,512,4096]{2,1,0:T(8,128)(2,1)} %all-gather.7.cloned.1.call-done) | copy-start | bytes 12582916
  77.4 153.9 %all-gather.11.cloned.1.call-start = ((), (), s32[]{:S(2)}) async-start(), calls=%async_computation.6 | async-start | bytes 8912896 | tf_op jit(solution)/shard_map/all_gather | solution.py:36
  78.1 231.5 %reduce-scatter.3.cloned.1.call-start = ((), (), s32[]{:S(2)}) async-start(), calls=%async_computation.2 | async-start | bytes 5242880 | tf_op jit(solution)/shard_map/reduce_scatter | solution.py:64
  257.5 52.0 %copy-start.1 = (bf16[1,512,1024]{2,1,0:T(8,128)(2,1)S(1)}, bf16[1,512,1024]{2,1,0:T(8,128)(2,1)}, u32[]{:S(2)}) copy-start(bf16[1,512,1024]{2,1,0:T(8,128)(2,1)} %param.8) | copy-start | bytes 3145732
  257.5 52.0 %copy-start.2 = (bf16[1,512,1024]{2,1,0:T(8,128)(2,1)S(1)}, bf16[1,512,1024]{2,1,0:T(8,128)(2,1)}, u32[]{:S(2)}) copy-start(bf16[1,512,1024]{2,1,0:T(8,128)(2,1)} %param.13) | copy-start | bytes 3145732
  264.2 105.2 %reduce-scatter.5.cloned.1.call-start = ((), (), s32[]{:S(2)}) async-start(), calls=%async_computation.3 | async-start | bytes 5242880 | tf_op jit(solution)/shard_map/reduce_scatter | solution.py:74
  312.4 84.0 %copy-start.3 = (bf16[512,1024]{1,0:T(8,128)(2,1)S(1)}, bf16[512,1024]{1,0:T(8,128)(2,1)}, u32[]{:S(2)}) copy-start(bf16[512,1024]{1,0:T(8,128)(2,1)} %reduce-scatter.3.cloned.1.call-done) | copy-start | bytes 3145732
  369.4 27.1 %collective-permute-start = (bf16[512,1024]{1,0:T(8,128)(2,1)}, bf16[512,1024]{1,0:T(8,128)(2,1)S(1)}, u32[]{:S(2)}, u32[]{:S(2)}) collective-permute-start(bf16[512,1024]{1,0:T(8,128)(2,1)} %reduce-scatter.5.cloned.1.call-done), channel_id=1, source_target_pairs={{0,64},{1,65},{2,66},{3,67},{4,68},{5,69},{6,70},{7,71},{8,72},{9,... | collective-permute-start | bytes 3145736 | tf_op jit(solution)/shard_map/ppermute | solution.py:12
Sparse Core Ops, SparseCore 0:
  9.0 50.6 all-gather.6
  77.5 76.6 all-gather.8
  156.4 74.7 all-gather.10
  264.3 45.1 reduce-scatter.2
  315.0 54.2 reduce-scatter.4
where the time goes:
time: 405 us
  waiting for transfers between devices  281 us (69%)
  matrix products  70.2 us (17%)
  other arithmetic  34.5 us (9%)
  between operations  13.2 us (3%)
  local copies, waits for them, and re-layouts  4.46 us (1%)
    all_gather x1, waiting for transfers between devices, body(): key_rows = lax.all_gather(projected[1], 'seq', axis=0, tiled=True)  75.9 us
    reduce_scatter x1, waiting for transfers between devices, body(): lax.psum_scatter(terms.astype(jnp.bfloat16), 'tp', scatter_dimension=1, t...  54.5 us
    all_gather x1, waiting for transfers between devices, body(): whole_rows = lax.all_gather(shard_rows, 'tp', axis=1, tiled=True)  51.4 us
    reduce_scatter x1, waiting for transfers between devices, body(): lax.psum_scatter(partial_value.astype(jnp.bfloat16), 'tp', scatter_dimens...  44.4 us
    all_gather x1, waiting for transfers between devices, body(): value_rows = lax.all_gather(projected[2], 'seq', axis=0, tiled=True)  27.5 us
    dot_general x1, matrix products, body(): jnp.einsum('thd,nhd->htn', query, key_rows, preferred_element_type=jnp.fl...  27.2 us
    dot_general x1, matrix products, body(): jnp.einsum('htn,nhd->htd', weights.astype(jnp.bfloat16), value_rows, pref...  26.3 us
    ppermute x1, waiting for transfers between devices, passed_along(): return lax.ppermute(value, axis, pairs)  25.8 us
  transfers between devices with their start and end apart: 6, of which 6 were waited for; matrix products, arithmetic and copies ran while one was open for 13% of the time, Pallas kernels for 0%

commit v1 on v0

v1 whole, which is shorter than its diff:
```python
import functools

import jax
import jax.numpy as jnp
from jax import lax
from jax.experimental import pallas as pl
from jax.experimental.pallas import tpu as pltpu
from jax.sharding import PartitionSpec as P

HEAD_DIM = 128
ROWS = 512
WIDE = 1024
COLS = 512
HEADS_HERE = 4
Q_SCALE = 1.4426950408889634 / HEAD_DIM**0.5
NT = (((1,), (1,)), ((), ()))
VMEM_LIMIT = 58 * 2**20


def cost(flops):
    return pl.CostEstimate(flops=int(flops), bytes_accessed=2**20, transcendentals=0)


def seq_pairs(move):
    where = [(h, z, c) for h in range(2) for z in range(4) for c in range(2)]
    index = lambda h, z, c: h * 8 + z * 2 + c
    return [(index(*p), index(*move(*p))) for p in where]


def along_z(value, by):
    return lax.ppermute(value, "seq", seq_pairs(lambda h, z, c: (h, (z + by) % 4, c)))


def across_x(value):
    return lax.ppermute(value, "seq", seq_pairs(lambda h, z, c: (1 - h, z, c)))


def across_cores(value):
    return lax.ppermute(value, "seq", seq_pairs(lambda h, z, c: (h, z, 1 - c)))


def along_y(value, by):
    return lax.ppermute(value, "tp", [(i, (i + by) % 4) for i in range(4)])


def after(value, *others):
    return lax.optimization_barrier((value, others))[0]


def gathered_y(value):
    one, three = along_y(value, 1), along_y(value, 3)
    return [one, along_y(value, 2), three]


def qkv_kernel(place, tokens, mod, weight, *rest):
    out, modulated, held, arrived, whole, landed = rest[-6:]
    z = place[1]
    rows = modulated.shape[0]
    quarter = rows // 4
    tile = 16
    lands = []
    for part in range(4):
        here = pl.ds(part * quarter, quarter)
        lands.append(pltpu.make_async_copy(tokens.at[here], whole.at[here], landed.at[part]))
    copies = []
    for c in range(3):
        for k in range(4):
            here = pl.ds(k * WIDE, WIDE)
            copies.append(
                pltpu.make_async_copy(weight.at[c, here], held.at[c, here], arrived.at[c * 4 + k])
            )
    for copy in lands + copies:
        copy.start()

    for first in range(0, rows, tile):
        if first % quarter == 0:
            lands[first // quarter].wait()
        here = pl.ds(first, tile)
        total = 0.0
        for k in range(4):
            part = whole[here, k * WIDE : (k + 1) * WIDE].astype(jnp.float32)
            total = total + jnp.sum(part, axis=1, keepdims=True)
        mean = total * (1.0 / (4 * WIDE))
        square = 0.0
        for k in range(4):
            part = whole[here, k * WIDE : (k + 1) * WIDE].astype(jnp.float32) - mean
            square = square + jnp.sum(part * part, axis=1, keepdims=True)
        scale = lax.rsqrt(square * (1.0 / (4 * WIDE)) + 1e-06)
        for k in range(4):
            columns = pl.ds(k * WIDE, WIDE)
            part = (whole[here, columns].astype(jnp.float32) - mean) * scale
            value = part * (1.0 + mod[1:2, columns]) + mod[0:1, columns]
            modulated[here, columns] = value.astype(jnp.bfloat16)

    for c in range(3):
        for copy in copies[c * 4 : c * 4 + 4]:
            copy.wait()
        product = jnp.dot(modulated[...], held[c], preferred_element_type=jnp.float32)
        if c == 0:
            product = product * Q_SCALE
        product = product.astype(jnp.bfloat16)
        for head in range(HEADS_HERE):
            slot = lax.rem(head + 4 - z, 4)
            out[slot, c] = product[:, head * HEAD_DIM : (head + 1) * HEAD_DIM]


def qkv(place, tokens, mod, weight, earlier):
    rows = tokens.shape[0]
    hbm = pl.BlockSpec(memory_space=pl.ANY)
    vmem = pl.BlockSpec(memory_space=pltpu.VMEM)
    return pl.pallas_call(
        qkv_kernel,
        in_specs=[pl.BlockSpec(memory_space=pltpu.SMEM), hbm, vmem, hbm] + [hbm] * len(earlier),
        out_specs=vmem,
        scratch_shapes=[
            pltpu.VMEM((rows, 4 * WIDE), jnp.bfloat16),
            pltpu.VMEM((3, 4 * WIDE, COLS), jnp.bfloat16),
            pltpu.SemaphoreType.DMA((12,)),
            pltpu.VMEM((rows, 4 * WIDE), jnp.bfloat16),
            pltpu.SemaphoreType.DMA((4,)),
        ],
        out_shape=jax.ShapeDtypeStruct((4, 3, rows, HEAD_DIM), jnp.bfloat16),
        compiler_params=pltpu.CompilerParams(vmem_limit_bytes=VMEM_LIMIT),
        cost_estimate=cost(2 * rows * 4 * WIDE * 3 * COLS),
        name="qkv",
    )(place, tokens, mod, weight, *earlier)


def attention_kernel(*refs, count, gates, first, last):
    query = refs[0][...]
    pairs = refs[1 : 1 + count]
    rest = refs[1 + count + gates :]
    rows = query.shape[0]
    step = 1024
    pieces = [(pair, at) for pair in pairs for at in range(0, pair.shape[1], step)]

    def scores_of(piece):
        pair, at = piece
        keys = pair[0, pl.ds(at, step), :]
        return lax.dot_general(query, keys, NT, preferred_element_type=jnp.float32)

    if first:
        top = jnp.full((rows, 1), -1e30, jnp.float32)
        total = jnp.zeros((rows, 1), jnp.float32)
        weighted = jnp.zeros((rows, HEAD_DIM), jnp.float32)
    else:
        weighted = rest[0][...]
        top = jnp.max(rest[1][...], axis=1, keepdims=True)
        total = jnp.max(rest[2][...], axis=1, keepdims=True)
        rest = rest[3:]
    ready = scores_of(pieces[0])
    for index, (pair, at) in enumerate(pieces):
        scores = ready
        if index + 1 < len(pieces):
            ready = scores_of(pieces[index + 1])
        new_top = jnp.maximum(top, jnp.max(scores, axis=1, keepdims=True))
        weights = jnp.exp2(scores - new_top)
        fade = jnp.exp2(top - new_top)
        total = total * fade + jnp.sum(weights, axis=1, keepdims=True)
        values = pair[1, pl.ds(at, step), :]
        update = jnp.dot(weights.astype(jnp.bfloat16), values, preferred_element_type=jnp.float32)
        weighted = weighted * fade + update
        top = new_top
    if last:
        rest[0][...] = (weighted / total).astype(jnp.bfloat16)
    else:
        rest[0][...] = weighted
        rest[1][...] = jnp.broadcast_to(top, (rows, HEAD_DIM))
        rest[2][...] = jnp.broadcast_to(total, (rows, HEAD_DIM))


def attention(query, pairs, carry, last, part, parts, earlier=()):
    rows = query.shape[0] // parts
    block = 512
    first = part * (rows // block)
    tokens = sum(pair.shape[1] for pair in pairs)
    row_block = pl.BlockSpec((block, HEAD_DIM), lambda i: (i, 0))
    in_block = pl.BlockSpec((block, HEAD_DIM), lambda i: (first + i, 0))
    shape = lambda dtype: jax.ShapeDtypeStruct((rows, HEAD_DIM), dtype)
    if last:
        out_shape, out_specs = shape(jnp.bfloat16), row_block
    else:
        out_shape, out_specs = [shape(jnp.float32)] * 3, [row_block] * 3
    return pl.pallas_call(
        functools.partial(attention_kernel, count=len(pairs), gates=len(earlier), first=not carry, last=last),
        grid=(rows // block,),
        in_specs=[in_block]
        + [pl.BlockSpec(pair.shape, lambda i: (0, 0, 0)) for pair in pairs]
        + [pl.BlockSpec(memory_space=pl.ANY)] * len(earlier)
        + [in_block] * len(carry),
        out_specs=out_specs,
        out_shape=out_shape,
        compiler_params=pltpu.CompilerParams(vmem_limit_bytes=VMEM_LIMIT),
        cost_estimate=pl.CostEstimate(
            flops=4 * rows * tokens * HEAD_DIM,
            bytes_accessed=4 * tokens * HEAD_DIM,
            transcendentals=rows * tokens,
        ),
        name="attention",
    )(query, *pairs, *earlier, *carry)


def output_kernel(place, *refs, addends, first, count):
    blocks, weights, scale, terms = refs[:4], refs[4 : 4 + count], refs[4 + count], refs[5 + count : -3]
    out, held, arrived = refs[-3:]
    y, z, branch, core, x_hi = place[0], place[1], place[2], place[3], place[4]
    rows = out.shape[0]
    copies = []
    for index in range(4):
        to = held.at[pl.ds(index * 4, 4)]
        source = weights[0].at[pl.ds(index * 4, 4)] if count == 1 else weights[index]
        copies.append(pltpu.make_async_copy(source, to, arrived.at[index]))
        copies[-1].start()

    def rows_of(back, by):
        row, head = lax.rem(y + 4 - back, 4), lax.rem(z + by, 4)
        if count == 1:
            return held[pl.ds(head * 4, 4), row].reshape(HEAD_DIM, WIDE)
        parts = []
        for i in range(4):
            across = lax.rem(head // 2 + x_hi, 2)
            behind = lax.rem(z + 4 - lax.rem(head, 2) * 2 - i // 2, 4)
            parts.append(held[lax.rem(i % 2 + core, 2) * 8 + across * 4 + behind, row])
        return jnp.concatenate(parts, axis=0)

    product = None
    for copy in copies:
        copy.wait()
    for back in range(4):
        share = jnp.concatenate([rows_of(back, by) for by in range(4)], axis=0)
        left = jnp.concatenate([blocks[back][by, pl.ds(first, rows), :] for by in range(4)], axis=1)
        update = jnp.dot(left, share, preferred_element_type=jnp.float32)
        product = update if product is None else product + update
    if addends == "early":
        out[...] = (product + terms[0][...].astype(jnp.float32)).astype(out.dtype)
    elif addends == "none":
        out[...] = product.astype(out.dtype)
    else:
        value = terms[0][...].astype(jnp.float32) + scale[0:1, :] * product
        out[...] = value + scale[1:2, :] * terms[1][...].astype(jnp.float32)
        half = terms[2].shape[0]
        early = terms[2][...].astype(jnp.float32)
        out[pl.ds(half, half), :] += branch.astype(jnp.float32) * early


def output(place, blocks, weights, scale, terms, addends, first, rows, dtype, name):
    vmem = pl.BlockSpec(memory_space=pltpu.VMEM)
    return pl.pallas_call(
        functools.partial(
            output_kernel, addends=addends, first=first, count=len(weights)
        ),
        in_specs=[pl.BlockSpec(memory_space=pltpu.SMEM)]
        + [vmem] * len(blocks)
        + [pl.BlockSpec(memory_space=pl.ANY)] * len(weights)
        + [vmem] * (1 + len(terms)),
        out_specs=vmem,
        scratch_shapes=[
            pltpu.VMEM((16, 4, 32, WIDE), jnp.bfloat16),
            pltpu.SemaphoreType.DMA((4,)),
        ],
        out_shape=jax.ShapeDtypeStruct((rows, WIDE), dtype),
        compiler_params=pltpu.CompilerParams(vmem_limit_bytes=VMEM_LIMIT),
        cost_estimate=cost(2 * rows * 2048 * WIDE),
        name=name,
    )(place, *blocks, *weights, scale, *terms)


def body(hidden, modulation, qkv_weight, out_weight, control_proj, cached_mlp):
    hidden, cached = hidden[0], cached_mlp[0]
    mod = modulation[0]
    branch = lax.axis_index("branch")
    y = lax.axis_index("tp")
    s = lax.axis_index("seq")
    z = lax.rem(s // 2, 4)
    place = jnp.stack([y, z, branch, lax.rem(s, 2), s // 8]).astype(jnp.int32)
    gates = lax.dynamic_slice_in_dim(mod[2:4], y * WIDE, WIDE, 1)
    turn = lambda by: lax.rem(y + by, 4)
    rows = ROWS // 2
    weight = qkv_weight[0].transpose(1, 0, 2)

    def sent_y(value):
        cut = lambda by: lax.dynamic_slice_in_dim(value, turn(by) * WIDE, WIDE, 1)
        return [cut(0)] + [along_y(cut(by), by) for by in (1, 2, 3)]

    def heads_turned(part):
        return [part[0]] + [along_z(part[by], by) for by in (1, 2, 3)]

    tokens = lax.all_gather(hidden, "tp", axis=1, tiled=True)

    with jax.named_scope("early_residual"):
        base = (hidden.astype(jnp.float32) + gates[1] * cached.astype(jnp.float32)).astype(jnp.bfloat16)
        sent = lax.ppermute(base[rows:], "branch", [(0, 1)])
        base = jnp.where(branch == 0, base[:rows], sent)

    with jax.named_scope("out_weight_columns"):
        share = lax.dynamic_slice_in_dim(out_weight[0], s * 32, 32, 0)
        turned = jnp.stack(sent_y(share))
        ordered = jnp.stack(
            [lax.dynamic_index_in_dim(turned, turn(4 - row), 0, keepdims=False) for row in range(4)]
        )
        of_z = jnp.stack([ordered] + [along_z(ordered, by) for by in (1, 2, 3)])

    with jax.named_scope("early_residual"):
        early = jnp.dot(base, control_proj, preferred_element_type=jnp.float32).astype(jnp.bfloat16)

    with jax.named_scope("joint_weight"):
        gated = (ordered.reshape(128, WIDE).astype(jnp.float32) * gates[0]).astype(jnp.bfloat16)
        joint = jnp.dot(gated, control_proj, preferred_element_type=jnp.float32).astype(jnp.bfloat16)

    with jax.named_scope("out_weight_columns"):
        of_x = across_x(after(of_z, sent))

    with jax.named_scope("joint_weight"):
        joint_share = lax.psum_scatter(joint, "tp", scatter_dimension=1, tiled=True)
    projected = qkv(place, tokens, mod, weight, [early, joint, of_x])
    with jax.named_scope("early_residual"):
        early = lax.psum_scatter(after(early, projected), "tp", scatter_dimension=1, tiled=True)

    turned = heads_turned(projected)
    with jax.named_scope("out_weight_columns"):
        mine = after([of_z, of_x], projected)
        out_columns = mine + [across_cores(part) for part in mine]
    query = jnp.concatenate([block[0] for block in turned], axis=0)
    near = jnp.concatenate([block[1:3] for block in turned], axis=1)
    far = across_x(near)
    carry = attention(query, [near, across_cores(near)], [], False, 0, 1, out_columns)
    far = after(far, carry)
    with jax.named_scope("joint_weight"):
        joint_share = after(joint_share, far, early).reshape(4, 32, WIDE)
        joint_columns = lax.all_gather(joint_share, "seq", axis=0)
    attended = attention(query, [far, across_cores(far)], carry, True, 0, 1)

    attended = attended.reshape(4, ROWS, HEAD_DIM)
    attended = jnp.stack([attended[0]] + [along_z(attended[by], 4 - by) for by in (1, 2, 3)])
    group = [attended, *gathered_y(attended)]
    joined = []
    for half in range(2):
        terms, kind = ([early], "early") if half == 0 else ([], "none")
        residual = output(
            place, group, [joint_columns], gates, terms, kind, half * rows, rows, jnp.bfloat16, "residual"
        )
        joined.append(lax.ppermute(residual, "branch", [(0, 1)]))
    terms = [hidden, cached, early]
    blended = output(
        place, group, out_columns, gates, terms, "blended", 0, ROWS, jnp.float32, "blended"
    )
    joined = jnp.concatenate(joined, axis=0)
    return (blended + joined.astype(jnp.float32)).astype(jnp.bfloat16)[None]


def solution(mesh):
    placed = (
        P("branch", "seq", "tp"),
        P("branch", None, None),
        P("branch", None, None, "tp"),
        P("branch", "tp", None),
        P("tp", None),
        P("branch", "seq", "tp"),
    )
    return jax.shard_map(
        body, mesh=mesh, in_specs=placed, out_specs=P("branch", "seq", "tp"), check_vma=False
    )
```

time: 405 us -> 235 us (0.58)
  waiting for transfers between devices: 281 us -> 91.5 us
  Pallas kernels: 0 us -> 64.4 us
  matrix products: 70.2 us -> 13.4 us
  starting transfers between devices: 1.62 us -> 35.4 us
  other arithmetic: 34.5 us -> 6.72 us
  local copies, waits for them, and re-layouts: 4.46 us -> 9.57 us
    all_gather x3 -> x2, waiting for transfers between devices: 155 us -> 0.57 us  [the longest x1 0.56 us: body(): joint_columns = lax.all_gather(joint_share, 'seq', axis=0)]
    reduce_scatter x2, waiting for transfers between devices: 98.9 us -> 0.01 us  [the longest x1 0.01 us: body(): lax.psum_scatter(after(early, projected), 'tp', scatter_dimension=1, tile...]
    ppermute x1 -> x24, waiting for transfers between devices: 25.8 us -> 90.2 us  [the longest x9 29.7 us: along_z(): lax.ppermute(value, 'seq', seq_pairs(lambda h, z, c: (h, (z + by) % 4, c)))]
    pallas_call x0 -> x6, Pallas kernels: none -> 64.4 us  [the longest x2 27.9 us: attention(): pl.pallas_call(functools.partial(attention_kernel, count=len(pairs), gate...]
    dot_general x4 -> x2, matrix products: 70.2 us -> 13.4 us  [the longest x1 7.38 us: body(): jnp.dot(base, control_proj, preferred_element_type=jnp.float32)]
    ppermute x1 -> x24, starting transfers between devices: 1.28 us -> 35.3 us  [the longest x9 17 us: along_z(): lax.ppermute(value, 'seq', seq_pairs(lambda h, z, c: (h, (z + by) % 4, c)))]
    reduce_sum x3 -> x0, other arithmetic: 28.7 us -> none  [the longest x1 22.3 us: body(): running_sum = jnp.sum(weights, axis=-1)]
    unnamed x8 -> x26, local copies, waits for them, and re-layouts: 0.02 us -> 4.87 us
  transfers between devices with their start and end apart: 6 -> 28, of which waited for: 6 -> 15; matrix products, arithmetic and copies ran while one was open for 13% -> 9% of each run, Pallas kernels for 0% -> 25%
where the time goes in v1:
time: 235 us; the launch traced here: 234 us
  waiting for transfers between devices  91.5 us (39%)
  Pallas kernels  64.4 us (27%)
  starting transfers between devices  35.4 us (15%)
  between operations  13.5 us (6%)
  matrix products  13.4 us (6%)
  local copies, waits for them, and re-layouts  9.57 us (4%)
  other arithmetic  6.72 us (3%)
    ppermute x9, waiting for transfers between devices, along_z(): lax.ppermute(value, 'seq', seq_pairs(lambda h, z, c: (h, (z + by) % 4, c)))  29.7 us
    pallas_call x2, Pallas kernels, attention(): pl.pallas_call(functools.partial(attention_kernel, count=len(pairs), gate...  27.9 us
    ppermute x2, waiting for transfers between devices, across_x(): return lax.ppermute(value, 'seq', seq_pairs(lambda h, z, c: (1 - h, z, c)))  24 us
    ppermute x6, waiting for transfers between devices, along_y(): return lax.ppermute(value, 'tp', [(i, (i + by) % 4) for i in range(4)])  23.5 us
    pallas_call x3, Pallas kernels, output(): pl.pallas_call(functools.partial(output_kernel, addends=addends, first=fi...  20.1 us
    ppermute x9, starting transfers between devices, along_z(): lax.ppermute(value, 'seq', seq_pairs(lambda h, z, c: (h, (z + by) % 4, c)))  17 us
    pallas_call x1, Pallas kernels, qkv(): pl.pallas_call(qkv_kernel, in_specs=[pl.BlockSpec(memory_space=pltpu.SMEM...  16.3 us
    ppermute x2, waiting for transfers between devices, body(): joined.append(lax.ppermute(residual, 'branch', [(0, 1)]))  10.3 us
  transfers between devices with their start and end apart: 28, of which 15 were waited for; matrix products, arithmetic and copies ran while one was open for 9% of the time, Pallas kernels for 25%

profile of v1, /device:TPU:2, one launch (start us, length us, event | category | flops | bytes accessed | tf_op | source)
XLA Modules:
  0.0 234.4 jit_solution(7997446692419890431)
XLA Ops:
  6.5 0.7 all-gather.6.cloned.1.call-update
  7.3 1.2 constant_dynamic-slice_fusion.6
  8.6 1.6 collective-permute-start.1
  10.2 1.7 collective-permute-start.3
  11.9 2.0 collective-permute-start.2
  13.8 0.9 slice.76
  14.7 0.1 constant_dynamic-slice_fusion
  14.8 1.6 add_convert_fusion.1
  16.5 1.3 collective-permute-start
  18.0 6.0 %convolution_convert_fusion.1.rest_1_ = bf16[128,4096]{1,0:T(8,128)(2,1)} fusion(bf16[1024,4096]{1,0:T(8,128)(2,1)} %param.10, bf16[128,1024]{1,0:T(8,128)(2,1)S(1)} %bitcast.62, f32[1024]{0:T(1024)S(1)} %bitcast.70), kind=kOutput, calls=%fused_computation.1 | convolution fusion | flops 1074659328 | bytes 9703424 | tf_op jit(solution)/shard_map/joint_weight/dot_general | solution.py:308
  24.1 4.2 %collective-permute-start.5 = (bf16[4,32,1024]{2,1,0:T(8,128)(2,1)S(1)}, bf16[4,32,1024]{2,1,0:T(8,128)(2,1)S(1)}, u32[]{:S(2)}, u32[]{:S(2)}) collective-permute-start(bf16[4,32,1024]{2,1,0:T(8,128)(2,1)S(1)} %get-tuple-element.35), channel_id=1, source_target_pairs={{0,16},{4,20},{8,24},{12,28},{16,0},{20,4},{24,8},{28,12},{32,48},... | collective-permute-start | bytes 786440 | tf_op jit(solution)/shard_map/out_weight_columns/ppermute | solution.py:31
  28.3 1.1 collective-permute-start.4
  29.4 2.1 collective-permute-start.6
  31.5 4.0 %collective-permute-done.5 = bf16[4,32,1024]{2,1,0:T(8,128)(2,1)S(1)} collective-permute-done((bf16[4,32,1024]{2,1,0:T(8,128)(2,1)S(1)}, bf16[4,32,1024]{2,1,0:T(8,128)(2,1)S(1)}, u32[]{:S(2)}, u32[]{:S(2)}) %collective-permute-start.5) | collective-permute-done | bytes 262176 | tf_op jit(solution)/shard_map/out_weight_columns/ppermute | solution.py:31
  35.5 3.5 %collective-permute-done.4 = bf16[4,32,1024]{2,1,0:T(8,128)(2,1)S(1)} collective-permute-done((bf16[4,32,1024]{2,1,0:T(8,128)(2,1)S(1)}, bf16[4,32,1024]{2,1,0:T(8,128)(2,1)S(1)}, u32[]{:S(2)}, u32[]{:S(2)}) %collective-permute-start.4) | collective-permute-done | bytes 262176 | tf_op jit(solution)/shard_map/out_weight_columns/ppermute | solution.py:31
  39.0 0.8 collective-permute-done.6
  39.8 0.1 pad_maximum_fusion.refs_3_.refs_4_
  40.0 2.4 %collective-permute-start.7 = (bf16[4,4,32,1024]{3,2,1,0:T(8,128)(2,1)S(1)}, bf16[4,4,32,1024]{3,2,1,0:T(8,128)(2,1)S(1)}, u32[]{:S(2)}, u32[]{:S(2)}) collective-permute-start(bf16[4,4,32,1024]{3,2,1,0:T(8,128)(2,1)S(1)} %pad_maximum_fusion.refs_3_.refs_4_), channel_id=1, source_target_pairs={{0,32},{4,36},{8,40},{12,44},{16,48},{20,52},{24,56},{28,60},{32,0... | collective-permute-start | bytes 3145736 | tf_op jit(solution)/shard_map/out_weight_columns/ppermute | solution.py:35
  42.3 0.6 stack.70.place
  42.9 7.4 %convolution_convert_fusion.rest_0_ = bf16[256,4096]{1,0:T(8,128)(2,1)} fusion(bf16[1024,4096]{1,0:T(8,128)(2,1)} %param.10, bf16[256,1024]{1,0:T(8,128)(2,1)} %collective-permute-done, bf16[512,1024]{1,0:T(8,128)(2,1)S(1)} %add_convert_fusion.1, pred[]{:T(512)S(6)} %eq.3), kind=kOutput, calls=%fused_computation | convolution fusion | flops 2148794368 | bytes 11534337 | tf_op jit(solution)/shard_map/early_residual/dot_general | solution.py:304
  50.3 14.9 %collective-permute-done.7.rest_2_.refs_4_.refs_5_ = bf16[4,4,32,1024]{3,2,1,0:T(8,128)(2,1)S(1)} collective-permute-done((bf16[4,4,32,1024]{3,2,1,0:T(8,128)(2,1)S(1)}, bf16[4,4,32,1024]{3,2,1,0:T(8,128)(2,1)S(1)}, u32[]{:S(2)}, u32[]{:S(2)}) %collective-permute-start.7) | collective-permute-done | bytes 1048608 | tf_op jit(solution)/shard_map/out_weight_columns/ppermute | solution.py:35
  65.2 1.0 copy-done.7
  66.2 16.3 %qkv.1 = bf16[4,3,512,128]{3,2,1,0:T(8,128)(2,1)} custom-call(s32[5]{0:T(128)} %stack.70.place, bf16[512,4096]{1,0:T(8,128)(2,1)} %bitcast.77, f32[4,4096]{1,0:T(4,128)} %bitcast.75, bf16[3,4096,512]{2,1,0:T(8,128)(2,1)} %bitcast.76, bf16[256,4096]{1,0:T(8,128)(2,1)} %convolution_convert_fusion.rest_0_, bf16[128,4096]{1,0:T(8,128)(2,1)} %convolution_convert_fusion.1.rest_1_, ...), custom_call_target="tpu_custom_call" | custom-call | flops 6442450944 | bytes 1048576 | tf_op jit(solution)/shard_map/qkv/pallas_call | solution.py:111
  82.6 1.3 copy-done.6
  83.9 0.1 slice_bitcast_fusion.2
  84.0 1.7 collective-permute-start.8
  85.8 2.0 collective-permute-start.10
  87.8 1.8 collective-permute-start.9
  89.6 0.5 collective-permute-start.14
  90.1 6.7 %collective-permute-done.8 = bf16[3,512,128]{2,1,0:T(8,128)(2,1)S(1)} collective-permute-done((bf16[3,512,128]{2,1,0:T(8,128)(2,1)S(1)}, bf16[3,512,128]{2,1,0:T(8,128)(2,1)S(1)}, u32[]{:S(2)}, u32[]{:S(2)}) %collective-permute-start.8) | collective-permute-done | bytes 393248 | tf_op jit(solution)/shard_map/ppermute | solution.py:31
  96.8 1.0 collective-permute-done.10
  97.8 7.0 %collective-permute-done.9 = bf16[3,512,128]{2,1,0:T(8,128)(2,1)S(1)} collective-permute-done((bf16[3,512,128]{2,1,0:T(8,128)(2,1)S(1)}, bf16[3,512,128]{2,1,0:T(8,128)(2,1)S(1)}, u32[]{:S(2)}, u32[]{:S(2)}) %collective-permute-start.9) | collective-permute-done | bytes 393248 | tf_op jit(solution)/shard_map/ppermute | solution.py:31
  104.8 1.1 pad_maximum_fusion.1.refs_1_
  105.9 2.3 %collective-permute-start.11 = (bf16[2,2048,128]{2,1,0:T(8,128)(2,1)}, bf16[2,2048,128]{2,1,0:T(8,128)(2,1)S(1)}, u32[]{:S(2)}, u32[]{:S(2)}) collective-permute-start(bf16[2,2048,128]{2,1,0:T(8,128)(2,1)} %pad_maximum_fusion.1.refs_1_), channel_id=1, source_target_pairs={{0,32},{4,36},{8,40},{12,44},{16,48},{20,52},{24,56},{28,60},{32,0... | collective-permute-start | bytes 3145736 | tf_op jit(solution)/shard_map/ppermute | solution.py:35
  108.3 0.8 pad_maximum_fusion.2.refs_0_
  109.2 1.1 copy-done.10
  110.2 0.3 copy-done.9
  110.5 13.9 %attention.2 = (f32[2048,128]{1,0:T(8,128)}, f32[2048,128]{1,0:T(8,128)}, f32[2048,128]{1,0:T(8,128)}) custom-call(bf16[2048,128]{1,0:T(8,128)(2,1)} %pad_maximum_fusion.2.refs_0_, bf16[2,2048,128]{2,1,0:T(8,128)(2,1)} %pad_maximum_fusion.1.refs_1_, bf16[2,2048,128]{2,1,0:T(8,128)(2,1)} %collective-permute-done.12.refs_2_, ...), custom_call_target="tpu_custom_call" | custom-call | flops 4294967296 | bytes 2097152 | tf_op jit(solution)/shard_map/attention/pallas_call | solution.py:184
  124.4 9.1 %collective-permute-done.11.refs_1_ = bf16[2,2048,128]{2,1,0:T(8,128)(2,1)S(1)} collective-permute-done((bf16[2,2048,128]{2,1,0:T(8,128)(2,1)}, bf16[2,2048,128]{2,1,0:T(8,128)(2,1)S(1)}, u32[]{:S(2)}, u32[]{:S(2)}) %collective-permute-start.11) | collective-permute-done | bytes 1048608 | tf_op jit(solution)/shard_map/ppermute | solution.py:35
  133.5 0.1 collective-permute-start.15
  133.6 2.6 %collective-permute-done.15.refs_2_ = bf16[2,2048,128]{2,1,0:T(8,128)(2,1)S(1)} collective-permute-done((bf16[2,2048,128]{2,1,0:T(8,128)(2,1)S(1)}, bf16[2,2048,128]{2,1,0:T(8,128)(2,1)S(1)}, u32[]{:S(2)}, u32[]{:S(2)}) %collective-permute-start.15) | collective-permute-done | bytes 1048608 | tf_op jit(solution)/shard_map/ppermute | solution.py:39
  136.3 1.0 copy-done.12
  137.3 14.1 %attention.3 = bf16[2048,128]{1,0:T(8,128)(2,1)} custom-call(bf16[2048,128]{1,0:T(8,128)(2,1)} %pad_maximum_fusion.2.refs_0_, bf16[2,2048,128]{2,1,0:T(8,128)(2,1)} %copy-done.11, bf16[2,2048,128]{2,1,0:T(8,128)(2,1)} %copy-done.12, f32[2048,128]{1,0:T(8,128)} %get-tuple-element.17.refs_3_, f32[2048,128]{1,0:T(8,128)} %get-tuple-element.18.refs_4_, ...), custom_call_target="tpu_custom_call" | custom-call | flops 4294967296 | bytes 2097152 | tf_op jit(solution)/shard_map/attention/pallas_call | solution.py:184
  151.3 1.1 slice_bitcast_fusion.4
  152.5 1.2 collective-permute-start.18
  153.7 2.2 collective-permute-start.17
  155.9 0.5 collective-permute-start.16
  156.4 4.2 %collective-permute-done.18 = bf16[512,128]{1,0:T(8,128)(2,1)S(1)} collective-permute-done((bf16[512,128]{1,0:T(8,128)(2,1)S(1)}, bf16[512,128]{1,0:T(8,128)(2,1)S(1)}, u32[]{:S(2)}, u32[]{:S(2)}) %collective-permute-start.18) | collective-permute-done | bytes 131104 | tf_op jit(solution)/shard_map/ppermute | solution.py:31
  160.6 2.6 %collective-permute-done.17 = bf16[512,128]{1,0:T(8,128)(2,1)S(1)} collective-permute-done((bf16[512,128]{1,0:T(8,128)(2,1)S(1)}, bf16[512,128]{1,0:T(8,128)(2,1)S(1)}, u32[]{:S(2)}, u32[]{:S(2)}) %collective-permute-start.17) | collective-permute-done | bytes 131104 | tf_op jit(solution)/shard_map/ppermute | solution.py:31
  163.3 1.8 collective-permute-start.21
  165.1 1.5 collective-permute-start.20
  166.6 0.6 collective-permute-start.19
  167.1 0.6 dynamic-slice_bitcast_fusion.3.refs_8_.refs_5_
  167.7 19.8 %collective-permute-done.21.refs_3_ = bf16[4,512,128]{2,1,0:T(8,128)(2,1)S(1)} collective-permute-done((bf16[4,512,128]{2,1,0:T(8,128)(2,1)S(1)}, bf16[4,512,128]{2,1,0:T(8,128)(2,1)S(1)}, u32[]{:S(2)}, u32[]{:S(2)}) %collective-permute-start.21) | collective-permute-done | bytes 524320 | tf_op jit(solution)/shard_map/ppermute | solution.py:43
  187.5 3.7 %collective-permute-done.19.refs_1_ = bf16[4,512,128]{2,1,0:T(8,128)(2,1)S(1)} collective-permute-done((bf16[4,512,128]{2,1,0:T(8,128)(2,1)S(1)}, bf16[4,512,128]{2,1,0:T(8,128)(2,1)S(1)}, u32[]{:S(2)}, u32[]{:S(2)}) %collective-permute-start.19) | collective-permute-done | bytes 524320 | tf_op jit(solution)/shard_map/ppermute | solution.py:43
  191.2 0.6 all-gather.4.cloned.1.call-done.refs_4_
  191.8 0.2 copy-done.4
  192.0 5.8 %residual.3 = bf16[256,1024]{1,0:T(8,128)(2,1)} custom-call(s32[5]{0:T(128)} %stack.70.place, bf16[4,512,128]{2,1,0:T(8,128)(2,1)} %copy-done.1, bf16[4,512,128]{2,1,0:T(8,128)(2,1)} %copy-done.4, bf16[4,512,128]{2,1,0:T(8,128)(2,1)} %copy-done.3, bf16[4,512,128]{2,1,0:T(8,128)(2,1)} %copy-done.2, ...), custom_call_target="tpu_custom_call" | custom-call | flops 1073741824 | bytes 1048576 | tf_op jit(solution)/shard_map/residual/pallas_call | solution.py:248
  197.8 1.3 collective-permute-start.23
  199.1 5.9 %residual.2 = bf16[256,1024]{1,0:T(8,128)(2,1)} custom-call(s32[5]{0:T(128)} %stack.70.place, bf16[4,512,128]{2,1,0:T(8,128)(2,1)} %copy-done.1, bf16[4,512,128]{2,1,0:T(8,128)(2,1)} %copy-done.4, bf16[4,512,128]{2,1,0:T(8,128)(2,1)} %copy-done.3, bf16[4,512,128]{2,1,0:T(8,128)(2,1)} %copy-done.2, ...), custom_call_target="tpu_custom_call" | custom-call | flops 1073741824 | bytes 1048576 | tf_op jit(solution)/shard_map/residual/pallas_call | solution.py:248
  205.0 1.3 collective-permute-start.22
  206.3 8.4 %blended.1 = f32[512,1024]{1,0:T(8,128)} custom-call(s32[5]{0:T(128)} %stack.70.place, bf16[4,512,128]{2,1,0:T(8,128)(2,1)} %copy-done.1, bf16[4,512,128]{2,1,0:T(8,128)(2,1)} %copy-done.4, bf16[4,512,128]{2,1,0:T(8,128)(2,1)} %copy-done.3, bf16[4,512,128]{2,1,0:T(8,128)(2,1)} %copy-done.2, bf16[4,4,32,1024]{3,2,1,0:T(8,128)(2,1)} %copy-done.5, ...), custom_call_target="tpu_custom_call" | custom-call | flops 2147483648 | bytes 1048576 | tf_op jit(solution)/shard_map/blended/pallas_call | solution.py:248
  214.7 10.3 %collective-permute-done.22 = bf16[256,1024]{1,0:T(8,128)(2,1)S(1)} collective-permute-done((bf16[256,1024]{1,0:T(8,128)(2,1)}, bf16[256,1024]{1,0:T(8,128)(2,1)S(1)}, u32[]{:S(2)}, u32[]{:S(2)}) %collective-permute-start.22) | collective-permute-done | bytes 524320 | tf_op jit(solution)/shard_map/ppermute | solution.py:342
  225.0 2.9 %fusion = bf16[1,512,1024]{2,1,0:T(8,128)(2,1)} fusion(f32[512,1024]{1,0:T(8,128)} %blended.1, bf16[256,1024]{1,0:T(8,128)(2,1)S(1)} %collective-permute-done.23, bf16[256,1024]{1,0:T(8,128)(2,1)S(1)} %collective-permute-done.22), kind=kLoop, calls=%fused_computation.4 | loop fusion | flops 3145728 | bytes 4194304 | tf_op jit(solution)/shard_map/broadcast_in_dim | solution.py:348
  (55 shorter events, 0.6 us)
Async XLA Ops:
  6.5 8.3 %copy-start = (bf16[1,512,1024]{2,1,0:T(8,128)(2,1)S(1)}, bf16[1,512,1024]{2,1,0:T(8,128)(2,1)}, u32[]{:S(2)}) copy-start(bf16[1,512,1024]{2,1,0:T(8,128)(2,1)} %param.6) | copy-start | bytes 3145732
  6.5 58.7 %all-gather.6.cloned.1.call-start = ((), (), s32[]{:S(2)}) async-start(), calls=%async_computation.5 | async-start | bytes 5242880 | tf_op jit(solution)/shard_map/all_gather | solution.py:288
  7.3 126.3 %reduce-scatter.5.cloned.1.call-start = ((), (), s32[]{:S(2)}) async-start(), calls=%async_computation.3 | async-start | bytes 1310720 | tf_op jit(solution)/shard_map/joint_weight/reduce_scatter | solution.py:314
  8.6 9.3 %collective-permute-start.1 = (bf16[32,1024]{1,0:T(8,128)(2,1)S(1)}, bf16[32,1024]{1,0:T(8,128)(2,1)S(1)}, u32[]{:S(2)}, u32[]{:S(2)}) collective-permute-start(bf16[32,1024]{1,0:T(8,128)(2,1)S(1)} %get-tuple-element.24), channel_id=1, source_target_pairs={{0,1},{1,2},{2,3},{3,0},{4,5},{5,6},{6,7},{7,4},{8,9},{9,10},{10,1... | collective-permute-start | bytes 196616 | tf_op jit(solution)/shard_map/out_weight_columns/ppermute | solution.py:43
  10.2 7.6 %collective-permute-start.3 = (bf16[32,1024]{1,0:T(8,128)(2,1)S(1)}, bf16[32,1024]{1,0:T(8,128)(2,1)S(1)}, u32[]{:S(2)}, u32[]{:S(2)}) collective-permute-start(bf16[32,1024]{1,0:T(8,128)(2,1)S(1)} %get-tuple-element.25), channel_id=1, source_target_pairs={{0,3},{1,0},{2,1},{3,2},{4,7},{5,4},{6,5},{7,6},{8,11},{9,8},{10,9... | collective-permute-start | bytes 196616 | tf_op jit(solution)/shard_map/out_weight_columns/ppermute | solution.py:43
  11.9 6.0 %collective-permute-start.2 = (bf16[32,1024]{1,0:T(8,128)(2,1)S(1)}, bf16[32,1024]{1,0:T(8,128)(2,1)S(1)}, u32[]{:S(2)}, u32[]{:S(2)}) collective-permute-start(bf16[32,1024]{1,0:T(8,128)(2,1)S(1)} %get-tuple-element.26), channel_id=1, source_target_pairs={{0,2},{1,3},{2,0},{3,1},{4,6},{5,7},{6,4},{7,5},{8,10},{9,11},{10,... | collective-permute-start | bytes 196616 | tf_op jit(solution)/shard_map/out_weight_columns/ppermute | solution.py:43
  16.5 23.5 %collective-permute-start = (bf16[256,1024]{1,0:T(8,128)(2,1)S(1)}, bf16[256,1024]{1,0:T(8,128)(2,1)}, u32[]{:S(2)}, u32[]{:S(2)}) collective-permute-start(bf16[256,1024]{1,0:T(8,128)(2,1)S(1)} %slice.99), channel_id=1, source_target_pairs={{0,64},{1,65},{2,66},{3,67},{4,68},{5,69},{6,70},{7,71},{8,72},{9,... | collective-permute-start | bytes 1572872 | tf_op jit(solution)/shard_map/early_residual/ppermute | solution.py:292
  24.0 109.5 %reduce-scatter.3.cloned.1.call-start = ((), (), s32[]{:S(2)}) async-start(), calls=%async_computation.2 | async-start | bytes 2621440 | tf_op jit(solution)/shard_map/early_residual/reduce_scatter | solution.py:317
  24.1 11.4 %collective-permute-start.5 = (bf16[4,32,1024]{2,1,0:T(8,128)(2,1)S(1)}, bf16[4,32,1024]{2,1,0:T(8,128)(2,1)S(1)}, u32[]{:S(2)}, u32[]{:S(2)}) collective-permute-start(bf16[4,32,1024]{2,1,0:T(8,128)(2,1)S(1)} %get-tuple-element.35), channel_id=1, source_target_pairs={{0,16},{4,20},{8,24},{12,28},{16,0},{20,4},{24,8},{28,12},{32,48},... | collective-permute-start | bytes 786440 | tf_op jit(solution)/shard_map/out_weight_columns/ppermute | solution.py:31
  28.3 10.7 %collective-permute-start.4 = (bf16[4,32,1024]{2,1,0:T(8,128)(2,1)S(1)}, bf16[4,32,1024]{2,1,0:T(8,128)(2,1)S(1)}, u32[]{:S(2)}, u32[]{:S(2)}) collective-permute-start(bf16[4,32,1024]{2,1,0:T(8,128)(2,1)S(1)} %get-tuple-element.35), channel_id=1, source_target_pairs={{0,8},{4,12},{8,16},{12,20},{16,24},{20,28},{24,0},{28,4},{32,40},... | collective-permute-start | bytes 786440 | tf_op jit(solution)/shard_map/out_weight_columns/ppermute | solution.py:31
  29.4 10.4 %collective-permute-start.6 = (bf16[4,32,1024]{2,1,0:T(8,128)(2,1)S(1)}, bf16[4,32,1024]{2,1,0:T(8,128)(2,1)S(1)}, u32[]{:S(2)}, u32[]{:S(2)}) collective-permute-start(bf16[4,32,1024]{2,1,0:T(8,128)(2,1)S(1)} %get-tuple-element.35), channel_id=1, source_target_pairs={{0,24},{4,28},{8,0},{12,4},{16,8},{20,12},{24,16},{28,20},{32,56},... | collective-permute-start | bytes 786440 | tf_op jit(solution)/shard_map/out_weight_columns/ppermute | solution.py:31
  40.0 49.6 %copy-start.5 = (bf16[4,4,32,1024]{3,2,1,0:T(8,128)(2,1)}, bf16[4,4,32,1024]{3,2,1,0:T(8,128)(2,1)S(1)}, u32[]{:S(2)}) copy-start(bf16[4,4,32,1024]{3,2,1,0:T(8,128)(2,1)S(1)} %pad_maximum_fusion.refs_3_.refs_4_) | copy-start | bytes 3145732
  40.0 25.2 %collective-permute-start.7 = (bf16[4,4,32,1024]{3,2,1,0:T(8,128)(2,1)S(1)}, bf16[4,4,32,1024]{3,2,1,0:T(8,128)(2,1)S(1)}, u32[]{:S(2)}, u32[]{:S(2)}) collective-permute-start(bf16[4,4,32,1024]{3,2,1,0:T(8,128)(2,1)S(1)} %pad_maximum_fusion.refs_3_.refs_4_), channel_id=1, source_target_pairs={{0,32},{4,36},{8,40},{12,44},{16,48},{20,52},{24,56},{28,60},{32,0... | collective-permute-start | bytes 3145736 | tf_op jit(solution)/shard_map/out_weight_columns/ppermute | solution.py:35
  65.2 1.0 copy-start.7
  82.5 1.4 copy-start.6
  82.6 109.2 %all-gather.4.cloned.1.call-start = ((), (), s32[]{:S(2)}) async-start(), calls=%async_computation.4 | async-start | bytes 4456448 | tf_op jit(solution)/shard_map/joint_weight/all_gather | solution.py:330
  83.9 5.6 %copy-start.8 = (bf16[4,4,32,1024]{3,2,1,0:T(8,128)(2,1)S(1)}, bf16[4,4,32,1024]{3,2,1,0:T(8,128)(2,1)}, u32[]{:S(2)}) copy-start(bf16[4,4,32,1024]{3,2,1,0:T(8,128)(2,1)} %copy-done.7) | copy-start | bytes 3145732
  84.0 12.8 %collective-permute-start.8 = (bf16[3,512,128]{2,1,0:T(8,128)(2,1)S(1)}, bf16[3,512,128]{2,1,0:T(8,128)(2,1)S(1)}, u32[]{:S(2)}, u32[]{:S(2)}) collective-permute-start(bf16[3,512,128]{2,1,0:T(8,128)(2,1)S(1)} %get-tuple-element.27), channel_id=1, source_target_pairs={{0,8},{4,12},{8,16},{12,20},{16,24},{20,28},{24,0},{28,4},{32,40},... | collective-permute-start | bytes 1179656 | tf_op jit(solution)/shard_map/ppermute | solution.py:31
  85.8 12.1 %collective-permute-start.10 = (bf16[3,512,128]{2,1,0:T(8,128)(2,1)S(1)}, bf16[3,512,128]{2,1,0:T(8,128)(2,1)S(1)}, u32[]{:S(2)}, u32[]{:S(2)}) collective-permute-start(bf16[3,512,128]{2,1,0:T(8,128)(2,1)S(1)} %get-tuple-element.28), channel_id=1, source_target_pairs={{0,24},{4,28},{8,0},{12,4},{16,8},{20,12},{24,16},{28,20},{32,56},... | collective-permute-start | bytes 1179656 | tf_op jit(solution)/shard_map/ppermute | solution.py:31
  87.8 17.1 %collective-permute-start.9 = (bf16[3,512,128]{2,1,0:T(8,128)(2,1)S(1)}, bf16[3,512,128]{2,1,0:T(8,128)(2,1)S(1)}, u32[]{:S(2)}, u32[]{:S(2)}) collective-permute-start(bf16[3,512,128]{2,1,0:T(8,128)(2,1)S(1)} %get-tuple-element.29), channel_id=1, source_target_pairs={{0,16},{4,20},{8,24},{12,28},{16,0},{20,4},{24,8},{28,12},{32,48},... | collective-permute-start | bytes 1179656 | tf_op jit(solution)/shard_map/ppermute | solution.py:31
  89.6 19.6 %collective-permute-start.13 = (bf16[4,4,32,1024]{3,2,1,0:T(8,128)(2,1)S(1)}, bf16[4,4,32,1024]{3,2,1,0:T(8,128)(2,1)S(1)}, u32[]{:S(2)}, u32[]{:S(2)}) collective-permute-start(bf16[4,4,32,1024]{3,2,1,0:T(8,128)(2,1)S(1)} %pad_maximum_fusion.refs_3_.refs_4_), channel_id=1, source_target_pairs={{0,4},{4,0},{8,12},{12,8},{16,20},{20,16},{24,28},{28,24},{32,36},... | collective-permute-start | bytes 3145736 | tf_op jit(solution)/shard_map/out_weight_columns/ppermute | solution.py:39
  89.6 19.6 %collective-permute-start.14 = (bf16[4,4,32,1024]{3,2,1,0:T(8,128)(2,1)S(1)}, bf16[4,4,32,1024]{3,2,1,0:T(8,128)(2,1)S(1)}, u32[]{:S(2)}, u32[]{:S(2)}) collective-permute-start(bf16[4,4,32,1024]{3,2,1,0:T(8,128)(2,1)S(1)} %copy-done.8), channel_id=1, source_target_pairs={{0,4},{4,0},{8,12},{12,8},{16,20},{20,16},{24,28},{28,24},{32,36},... | collective-permute-start | bytes 3145736 | tf_op jit(solution)/shard_map/out_weight_columns/ppermute | solution.py:39
  105.9 4.3 %collective-permute-start.12 = (bf16[2,2048,128]{2,1,0:T(8,128)(2,1)}, bf16[2,2048,128]{2,1,0:T(8,128)(2,1)}, u32[]{:S(2)}, u32[]{:S(2)}) collective-permute-start(bf16[2,2048,128]{2,1,0:T(8,128)(2,1)} %pad_maximum_fusion.1.refs_1_), channel_id=1, source_target_pairs={{0,4},{4,0},{8,12},{12,8},{16,20},{20,16},{24,28},{28,24},{32,36},... | collective-permute-start | bytes 3145736 | tf_op jit(solution)/shard_map/ppermute | solution.py:39
  105.9 27.6 %collective-permute-start.11 = (bf16[2,2048,128]{2,1,0:T(8,128)(2,1)}, bf16[2,2048,128]{2,1,0:T(8,128)(2,1)S(1)}, u32[]{:S(2)}, u32[]{:S(2)}) collective-permute-start(bf16[2,2048,128]{2,1,0:T(8,128)(2,1)} %pad_maximum_fusion.1.refs_1_), channel_id=1, source_target_pairs={{0,32},{4,36},{8,40},{12,44},{16,48},{20,52},{24,56},{28,60},{32,0... | collective-permute-start | bytes 3145736 | tf_op jit(solution)/shard_map/ppermute | solution.py:35
  109.1 1.4 copy-start.9
  109.1 1.1 copy-start.10
  133.5 2.8 %copy-start.11 = (bf16[2,2048,128]{2,1,0:T(8,128)(2,1)}, bf16[2,2048,128]{2,1,0:T(8,128)(2,1)S(1)}, u32[]{:S(2)}) copy-start(bf16[2,2048,128]{2,1,0:T(8,128)(2,1)S(1)} %collective-permute-done.11.refs_1_) | copy-start | bytes 3145732
  133.5 2.7 %collective-permute-start.15 = (bf16[2,2048,128]{2,1,0:T(8,128)(2,1)S(1)}, bf16[2,2048,128]{2,1,0:T(8,128)(2,1)S(1)}, u32[]{:S(2)}, u32[]{:S(2)}) collective-permute-start(bf16[2,2048,128]{2,1,0:T(8,128)(2,1)S(1)} %collective-permute-done.11.refs_1_), channel_id=1, source_target_pairs={{0,4},{4,0},{8,12},{12,8},{16,20},{20,16},{24,28},{28,24},{32,36},... | collective-permute-start | bytes 3145736 | tf_op jit(solution)/shard_map/ppermute | solution.py:39
  136.3 1.0 copy-start.12
  152.5 8.1 %collective-permute-start.18 = (bf16[512,128]{1,0:T(8,128)(2,1)S(1)}, bf16[512,128]{1,0:T(8,128)(2,1)S(1)}, u32[]{:S(2)}, u32[]{:S(2)}) collective-permute-start(bf16[512,128]{1,0:T(8,128)(2,1)S(1)} %get-tuple-element.31), channel_id=1, source_target_pairs={{0,8},{4,12},{8,16},{12,20},{16,24},{20,28},{24,0},{28,4},{32,40},... | collective-permute-start | bytes 393224 | tf_op jit(solution)/shard_map/ppermute | solution.py:31
  153.7 9.5 %collective-permute-start.17 = (bf16[512,128]{1,0:T(8,128)(2,1)S(1)}, bf16[512,128]{1,0:T(8,128)(2,1)S(1)}, u32[]{:S(2)}, u32[]{:S(2)}) collective-permute-start(bf16[512,128]{1,0:T(8,128)(2,1)S(1)} %get-tuple-element.32), channel_id=1, source_target_pairs={{0,16},{4,20},{8,24},{12,28},{16,0},{20,4},{24,8},{28,12},{32,48},... | collective-permute-start | bytes 393224 | tf_op jit(solution)/shard_map/ppermute | solution.py:31
  155.9 7.3 %collective-permute-start.16 = (bf16[512,128]{1,0:T(8,128)(2,1)S(1)}, bf16[512,128]{1,0:T(8,128)(2,1)S(1)}, u32[]{:S(2)}, u32[]{:S(2)}) collective-permute-start(bf16[512,128]{1,0:T(8,128)(2,1)S(1)} %get-tuple-element.33), channel_id=1, source_target_pairs={{0,24},{4,28},{8,0},{12,4},{16,8},{20,12},{24,16},{28,20},{32,56},... | collective-permute-start | bytes 393224 | tf_op jit(solution)/shard_map/ppermute | solution.py:31
  163.3 28.5 %copy-start.1 = (bf16[4,512,128]{2,1,0:T(8,128)(2,1)}, bf16[4,512,128]{2,1,0:T(8,128)(2,1)S(1)}, u32[]{:S(2)}) copy-start(bf16[4,512,128]{2,1,0:T(8,128)(2,1)S(1)} %pad_maximum_fusion.3.refs_0_) | copy-start | bytes 1572868
  163.3 24.3 %collective-permute-start.21 = (bf16[4,512,128]{2,1,0:T(8,128)(2,1)S(1)}, bf16[4,512,128]{2,1,0:T(8,128)(2,1)S(1)}, u32[]{:S(2)}, u32[]{:S(2)}) collective-permute-start(bf16[4,512,128]{2,1,0:T(8,128)(2,1)S(1)} %pad_maximum_fusion.3.refs_0_), channel_id=1, source_target_pairs={{0,3},{1,0},{2,1},{3,2},{4,7},{5,4},{6,5},{7,6},{8,11},{9,8},{10,9... | collective-permute-start | bytes 1572872 | tf_op jit(solution)/shard_map/ppermute | solution.py:43
  165.1 22.4 %collective-permute-start.20 = (bf16[4,512,128]{2,1,0:T(8,128)(2,1)S(1)}, bf16[4,512,128]{2,1,0:T(8,128)(2,1)S(1)}, u32[]{:S(2)}, u32[]{:S(2)}) collective-permute-start(bf16[4,512,128]{2,1,0:T(8,128)(2,1)S(1)} %pad_maximum_fusion.3.refs_0_), channel_id=1, source_target_pairs={{0,2},{1,3},{2,0},{3,1},{4,6},{5,7},{6,4},{7,5},{8,10},{9,11},{10,... | collective-permute-start | bytes 1572872 | tf_op jit(solution)/shard_map/ppermute | solution.py:43
  166.6 24.6 %collective-permute-start.19 = (bf16[4,512,128]{2,1,0:T(8,128)(2,1)S(1)}, bf16[4,512,128]{2,1,0:T(8,128)(2,1)S(1)}, u32[]{:S(2)}, u32[]{:S(2)}) collective-permute-start(bf16[4,512,128]{2,1,0:T(8,128)(2,1)S(1)} %pad_maximum_fusion.3.refs_0_), channel_id=1, source_target_pairs={{0,1},{1,2},{2,3},{3,0},{4,5},{5,6},{6,7},{7,4},{8,9},{9,10},{10,1... | collective-permute-start | bytes 1572872 | tf_op jit(solution)/shard_map/ppermute | solution.py:43
  187.5 4.2 %copy-start.2 = (bf16[4,512,128]{2,1,0:T(8,128)(2,1)}, bf16[4,512,128]{2,1,0:T(8,128)(2,1)S(1)}, u32[]{:S(2)}) copy-start(bf16[4,512,128]{2,1,0:T(8,128)(2,1)S(1)} %collective-permute-done.21.refs_3_) | copy-start | bytes 1572868
  187.5 4.2 %copy-start.3 = (bf16[4,512,128]{2,1,0:T(8,128)(2,1)}, bf16[4,512,128]{2,1,0:T(8,128)(2,1)S(1)}, u32[]{:S(2)}) copy-start(bf16[4,512,128]{2,1,0:T(8,128)(2,1)S(1)} %collective-permute-done.20.refs_2_) | copy-start | bytes 1572868
  191.2 0.8 copy-start.4
  197.8 16.9 %collective-permute-start.23 = (bf16[256,1024]{1,0:T(8,128)(2,1)}, bf16[256,1024]{1,0:T(8,128)(2,1)S(1)}, u32[]{:S(2)}, u32[]{:S(2)}) collective-permute-start(bf16[256,1024]{1,0:T(8,128)(2,1)} %residual.3), channel_id=1, source_target_pairs={{0,64},{1,65},{2,66},{3,67},{4,68},{5,69},{6,70},{7,71},{8,72},{9,... | collective-permute-start | bytes 1572872 | tf_op jit(solution)/shard_map/ppermute | solution.py:342
  205.0 20.0 %collective-permute-start.22 = (bf16[256,1024]{1,0:T(8,128)(2,1)}, bf16[256,1024]{1,0:T(8,128)(2,1)S(1)}, u32[]{:S(2)}, u32[]{:S(2)}) collective-permute-start(bf16[256,1024]{1,0:T(8,128)(2,1)} %residual.2), channel_id=1, source_target_pairs={{0,64},{1,65},{2,66},{3,67},{4,68},{5,69},{6,70},{7,71},{8,72},{9,... | collective-permute-start | bytes 1572872 | tf_op jit(solution)/shard_map/ppermute | solution.py:342
Sparse Core Ops, SparseCore 0:
  9.0 50.6 all-gather.5
  62.1 23.8 reduce-scatter.4
  88.6 29.3 reduce-scatter.2
  133.7 58.0 all-gather.3

commit v2 on v1

--- a/solution.py
+++ b/solution.py
@@ -69,12 +69,15 @@
             copies.append(
                 pltpu.make_async_copy(weight.at[c, here], held.at[c, here], arrived.at[c * 4 + k])
             )
-    for copy in lands + copies:
+    for copy in lands + copies[:4]:
         copy.start()
 
     for first in range(0, rows, tile):
         if first % quarter == 0:
             lands[first // quarter].wait()
+            if first // quarter in (1, 2):
+                for copy in copies[first // quarter * 4 : first // quarter * 4 + 4]:
+                    copy.start()
         here = pl.ds(first, tile)
         total = 0.0
         for k in range(4):
@@ -126,17 +129,40 @@
     )(place, tokens, mod, weight, *earlier)
 
 
+def products_kernel(one, two, right, out_one, out_two):
+    for left, out in ((one, out_one), (two, out_two)):
+        out[...] = jnp.dot(left[...], right[...], preferred_element_type=jnp.float32).astype(out.dtype)
+
+
+def products(one, two, right):
+    depth, columns = right.shape
+    rows = (one.shape[0], two.shape[0])
+    return pl.pallas_call(
+        products_kernel,
+        grid=(columns // WIDE,),
+        in_specs=[pl.BlockSpec((count, depth), lambda n: (0, 0)) for count in rows]
+        + [pl.BlockSpec((depth, WIDE), lambda n: (0, n))],
+        out_specs=[pl.BlockSpec((count, WIDE), lambda n: (0, n)) for count in rows],
+        out_shape=[jax.ShapeDtypeStruct((count, columns), jnp.bfloat16) for count in rows],
+        compiler_params=pltpu.CompilerParams(vmem_limit_bytes=VMEM_LIMIT),
+        cost_estimate=cost(2 * sum(rows) * depth * columns),
+        name="products",
+    )(one, two, right)
+
+
 def attention_kernel(*refs, count, gates, first, last):
     query = refs[0][...]
     pairs = refs[1 : 1 + count]
     rest = refs[1 + count + gates :]
     rows = query.shape[0]
-    step = 1024
-    pieces = [(pair, at) for pair in pairs for at in range(0, pair.shape[1], step)]
+    pieces = []
+    for pair in pairs:
+        step = pair.shape[1] // pl.cdiv(pair.shape[1], 1024)
+        pieces += [(pair, pl.ds(at, step)) for at in range(0, pair.shape[1], step)]
 
     def scores_of(piece):
         pair, at = piece
-        keys = pair[0, pl.ds(at, step), :]
+        keys = pair[0, at, :]
         return lax.dot_general(query, keys, NT, preferred_element_type=jnp.float32)
 
     if first:
@@ -157,7 +183,7 @@
         weights = jnp.exp2(scores - new_top)
         fade = jnp.exp2(top - new_top)
         total = total * fade + jnp.sum(weights, axis=1, keepdims=True)
-        values = pair[1, pl.ds(at, step), :]
+        values = pair[1, at, :]
         update = jnp.dot(weights.astype(jnp.bfloat16), values, preferred_element_type=jnp.float32)
         weighted = weighted * fade + update
         top = new_top
@@ -200,15 +226,17 @@
     )(query, *pairs, *earlier, *carry)
 
 
-def output_kernel(place, *refs, addends, first, count):
-    blocks, weights, scale, terms = refs[:4], refs[4 : 4 + count], refs[4 + count], refs[5 + count : -3]
+def output_kernel(place, *refs, groups, count):
+    blocks, refs = refs[: 4 * groups], refs[4 * groups :]
+    weights, scale, terms = refs[:count], refs[count], refs[count + 1 : -3]
     out, held, arrived = refs[-3:]
     y, z, branch, core, x_hi = place[0], place[1], place[2], place[3], place[4]
     rows = out.shape[0]
     copies = []
     for index in range(4):
         to = held.at[pl.ds(index * 4, 4)]
-        source = weights[0].at[pl.ds(index * 4, 4)] if count == 1 else weights[index]
+        per = 4 // count
+        source = weights[index // per].at[pl.ds(index % per * 4, 4)]
         copies.append(pltpu.make_async_copy(source, to, arrived.at[index]))
         copies[-1].start()
 
@@ -220,34 +248,41 @@
         for i in range(4):
             across = lax.rem(head // 2 + x_hi, 2)
             behind = lax.rem(z + 4 - lax.rem(head, 2) * 2 - i // 2, 4)
-            parts.append(held[lax.rem(i % 2 + core, 2) * 8 + across * 4 + behind, row])
+            parts.append(held[lax.rem(i % 2 + core, 2) * 8 + behind * 2 + across, row])
         return jnp.concatenate(parts, axis=0)
 
-    product = None
     for copy in copies:
         copy.wait()
+    products = [None] * groups
     for back in range(4):
         share = jnp.concatenate([rows_of(back, by) for by in range(4)], axis=0)
-        left = jnp.concatenate([blocks[back][by, pl.ds(first, rows), :] for by in range(4)], axis=1)
-        update = jnp.dot(left, share, preferred_element_type=jnp.float32)
-        product = update if product is None else product + update
-    if addends == "early":
-        out[...] = (product + terms[0][...].astype(jnp.float32)).astype(out.dtype)
-    elif addends == "none":
+        for group in range(groups):
+            block = blocks[4 * group + back]
+            left = jnp.concatenate([block[by] for by in range(4)], axis=1)
+            update = jnp.dot(left, share, preferred_element_type=jnp.float32)
+            products[group] = update if back == 0 else products[group] + update
+    if count == 1:
+        product = products[0]
+        if terms:
+            product = product + terms[0][...].astype(jnp.float32)
         out[...] = product.astype(out.dtype)
     else:
-        value = terms[0][...].astype(jnp.float32) + scale[0:1, :] * product
-        out[...] = value + scale[1:2, :] * terms[1][...].astype(jnp.float32)
-        half = terms[2].shape[0]
-        early = terms[2][...].astype(jnp.float32)
-        out[pl.ds(half, half), :] += branch.astype(jnp.float32) * early
-
-
-def output(place, blocks, weights, scale, terms, addends, first, rows, dtype, name):
+        for group in range(groups):
+            here = pl.ds(group * (rows // groups), rows // groups)
+            value = terms[0][here, :].astype(jnp.float32) + scale[0:1, :] * products[group]
+            value = value + scale[1:2, :] * terms[1][here, :].astype(jnp.float32)
+            if group == 1:
+                value = value + branch.astype(jnp.float32) * terms[2][...].astype(jnp.float32)
+            out[here, :] = value
+
+
+def output(place, groups, weights, scale, terms, dtype, name):
+    rows = groups[0][0].shape[1] * len(groups)
+    blocks = [block for group in groups for block in group]
     vmem = pl.BlockSpec(memory_space=pltpu.VMEM)
     return pl.pallas_call(
         functools.partial(
-            output_kernel, addends=addends, first=first, count=len(weights)
+            output_kernel, groups=len(groups), count=len(weights)
         ),
         in_specs=[pl.BlockSpec(memory_space=pltpu.SMEM)]
         + [vmem] * len(blocks)
@@ -287,63 +322,54 @@
 
     tokens = lax.all_gather(hidden, "tp", axis=1, tiled=True)
 
-    with jax.named_scope("early_residual"):
-        base = (hidden.astype(jnp.float32) + gates[1] * cached.astype(jnp.float32)).astype(jnp.bfloat16)
-        sent = lax.ppermute(base[rows:], "branch", [(0, 1)])
-        base = jnp.where(branch == 0, base[:rows], sent)
-
     with jax.named_scope("out_weight_columns"):
         share = lax.dynamic_slice_in_dim(out_weight[0], s * 32, 32, 0)
         turned = jnp.stack(sent_y(share))
         ordered = jnp.stack(
             [lax.dynamic_index_in_dim(turned, turn(4 - row), 0, keepdims=False) for row in range(4)]
         )
-        of_z = jnp.stack([ordered] + [along_z(ordered, by) for by in (1, 2, 3)])
-
+        of_x = jnp.stack([ordered, across_x(ordered)])
+        of_xz = [of_x] + [along_z(of_x, by) for by in (1, 2, 3)]
+
+    base = (hidden.astype(jnp.float32) + gates[1] * cached.astype(jnp.float32)).astype(jnp.bfloat16)
+    sent = lax.ppermute(base[rows:], "branch", [(0, 1)])
+    base = after(jnp.where(branch == 0, base[:rows], sent), *of_xz)
+    gated = (ordered.reshape(128, WIDE).astype(jnp.float32) * gates[0]).astype(jnp.bfloat16)
+    joint, early = products(gated, base, control_proj)
+    joint_share = lax.psum_scatter(joint, "tp", scatter_dimension=1, tiled=True)
+
+    projected = qkv(place, tokens, mod, weight, [joint, early])
     with jax.named_scope("early_residual"):
-        early = jnp.dot(base, control_proj, preferred_element_type=jnp.float32).astype(jnp.bfloat16)
-
-    with jax.named_scope("joint_weight"):
-        gated = (ordered.reshape(128, WIDE).astype(jnp.float32) * gates[0]).astype(jnp.bfloat16)
-        joint = jnp.dot(gated, control_proj, preferred_element_type=jnp.float32).astype(jnp.bfloat16)
-
-    with jax.named_scope("out_weight_columns"):
-        of_x = across_x(after(of_z, sent))
-
-    with jax.named_scope("joint_weight"):
-        joint_share = lax.psum_scatter(joint, "tp", scatter_dimension=1, tiled=True)
-    projected = qkv(place, tokens, mod, weight, [early, joint, of_x])
-    with jax.named_scope("early_residual"):
-        early = lax.psum_scatter(after(early, projected), "tp", scatter_dimension=1, tiled=True)
+        early = lax.psum_scatter(early, "tp", scatter_dimension=1, tiled=True)
+
 
     turned = heads_turned(projected)
     with jax.named_scope("out_weight_columns"):
-        mine = after([of_z, of_x], projected)
-        out_columns = mine + [across_cores(part) for part in mine]
+        of_xz = jnp.stack(after(of_xz, projected)).reshape(8, 4, 32, WIDE)
+        out_columns = [of_xz, across_cores(of_xz)]
     query = jnp.concatenate([block[0] for block in turned], axis=0)
     near = jnp.concatenate([block[1:3] for block in turned], axis=1)
     far = across_x(near)
     carry = attention(query, [near, across_cores(near)], [], False, 0, 1, out_columns)
     far = after(far, carry)
     with jax.named_scope("joint_weight"):
-        joint_share = after(joint_share, far, early).reshape(4, 32, WIDE)
+        joint_share = after(joint_share, near).reshape(4, 32, WIDE)
         joint_columns = lax.all_gather(joint_share, "seq", axis=0)
-    attended = attention(query, [far, across_cores(far)], carry, True, 0, 1)
+    attended = attention(query, [far, across_cores(far)], carry, True, 0, 1, [early])
 
     attended = attended.reshape(4, ROWS, HEAD_DIM)
-    attended = jnp.stack([attended[0]] + [along_z(attended[by], 4 - by) for by in (1, 2, 3)])
-    group = [attended, *gathered_y(attended)]
+    attended = [attended[0]] + [along_z(attended[by], 4 - by) for by in (1, 2, 3)]
+    halves = []
+    for half in range(2):
+        part = jnp.stack([block[half * rows : (half + 1) * rows] for block in attended])
+        halves.append([part, *gathered_y(part)])
     joined = []
     for half in range(2):
-        terms, kind = ([early], "early") if half == 0 else ([], "none")
-        residual = output(
-            place, group, [joint_columns], gates, terms, kind, half * rows, rows, jnp.bfloat16, "residual"
-        )
+        terms = [early] if half == 0 else []
+        residual = output(place, halves[half : half + 1], [joint_columns], gates, terms, jnp.bfloat16, "residual")
         joined.append(lax.ppermute(residual, "branch", [(0, 1)]))
     terms = [hidden, cached, early]
-    blended = output(
-        place, group, out_columns, gates, terms, "blended", 0, ROWS, jnp.float32, "blended"
-    )
+    blended = output(place, halves, out_columns, gates, terms, jnp.float32, "blended")
     joined = jnp.concatenate(joined, axis=0)
     return (blended + joined.astype(jnp.float32)).astype(jnp.bfloat16)[None]
 

time: 235 us -> 223 us (0.949)
  waiting for transfers between devices: 91.5 us -> 78.1 us
  matrix products: 13.4 us -> 0 us
  local copies, waits for them, and re-layouts: 9.57 us -> 16.9 us
  Pallas kernels: 64.4 us -> 68.8 us
    ppermute x2, waiting for transfers between devices: 24 us -> 9.92 us  [across_x(): return lax.ppermute(value, 'seq', seq_pairs(lambda h, z, c: (1 - h, z, c)))]
    dot_general x2 -> x0, matrix products: 13.4 us -> none  [the longest x1 7.38 us: body(): jnp.dot(base, control_proj, preferred_element_type=jnp.float32)]
    ppermute x9, waiting for transfers between devices: 29.7 us -> 39.8 us  [along_z(): lax.ppermute(value, 'seq', seq_pairs(lambda h, z, c: (h, (z + by) % 4, c)))]
    ppermute x6 -> x9, waiting for transfers between devices: 23.5 us -> 14.1 us  [along_y(): return lax.ppermute(value, 'tp', [(i, (i + by) % 4) for i in range(4)])]
    pallas_call x3 -> x4, Pallas kernels: 20.1 us -> 27 us  [the longest x3 19.4 us: output(): pl.pallas_call(functools.partial(output_kernel, groups=len(groups), count...]
    ppermute x2, waiting for transfers between devices: 10.3 us -> 6.09 us  [body(): joined.append(lax.ppermute(residual, 'branch', [(0, 1)]))]
    ppermute x1, waiting for transfers between devices: 0.01 us -> 3.84 us  [body(): sent = lax.ppermute(base[rows:], 'branch', [(0, 1)])]
    ppermute x6 -> x9, starting transfers between devices: 9.17 us -> 12.3 us  [along_y(): return lax.ppermute(value, 'tp', [(i, (i + by) % 4) for i in range(4)])]
  transfers between devices with their start and end apart: 28 -> 30, of which waited for: 15 -> 18; matrix products, arithmetic and copies ran while one was open for 9% -> 7% of each run, Pallas kernels for 25% -> 31%
where the time goes in v2:
time: 223 us; the launch traced here: 221 us
  waiting for transfers between devices  78.1 us (35%)
  Pallas kernels  68.8 us (31%)
  starting transfers between devices  35.6 us (16%)
  local copies, waits for them, and re-layouts  16.9 us (8%)
  between operations  13.6 us (6%)
  other arithmetic  7.93 us (4%)
    ppermute x9, waiting for transfers between devices, along_z(): lax.ppermute(value, 'seq', seq_pairs(lambda h, z, c: (h, (z + by) % 4, c)))  39.8 us
    pallas_call x2, Pallas kernels, attention(): pl.pallas_call(functools.partial(attention_kernel, count=len(pairs), gate...  27.9 us
    pallas_call x3, Pallas kernels, output(): pl.pallas_call(functools.partial(output_kernel, groups=len(groups), count...  19.4 us
    ppermute x9, waiting for transfers between devices, along_y(): return lax.ppermute(value, 'tp', [(i, (i + by) % 4) for i in range(4)])  14.1 us
    ppermute x9, starting transfers between devices, along_z(): lax.ppermute(value, 'seq', seq_pairs(lambda h, z, c: (h, (z + by) % 4, c)))  14 us
    pallas_call x1, Pallas kernels, qkv(): pl.pallas_call(qkv_kernel, in_specs=[pl.BlockSpec(memory_space=pltpu.SMEM...  13.8 us
    ppermute x9, starting transfers between devices, along_y(): return lax.ppermute(value, 'tp', [(i, (i + by) % 4) for i in range(4)])  12.3 us
    ppermute x2, waiting for transfers between devices, across_x(): return lax.ppermute(value, 'seq', seq_pairs(lambda h, z, c: (1 - h, z, c)))  9.92 us
  transfers between devices with their start and end apart: 30, of which 18 were waited for; matrix products, arithmetic and copies ran while one was open for 7% of the time, Pallas kernels for 31%

profile of v2, /device:TPU:2, one launch (start us, length us, event | category | flops | bytes accessed | tf_op | source)
XLA Modules:
  0.0 220.8 jit_solution(16691311839608335943)
XLA Ops:
  6.5 0.7 all-gather.6.cloned.1.call-update
  7.4 1.2 constant_dynamic-slice_fusion.6
  8.6 1.6 collective-permute-start
  10.2 2.9 %collective-permute-start.1 = (bf16[32,1024]{1,0:T(8,128)(2,1)S(1)}, bf16[32,1024]{1,0:T(8,128)(2,1)S(1)}, u32[]{:S(2)}, u32[]{:S(2)}) collective-permute-start(bf16[32,1024]{1,0:T(8,128)(2,1)S(1)} %get-tuple-element.32), channel_id=1, source_target_pairs={{0,2},{1,3},{2,0},{3,1},{4,6},{5,7},{6,4},{7,5},{8,10},{9,11},{10,... | collective-permute-start | bytes 196616 | tf_op jit(solution)/shard_map/out_weight_columns/ppermute | solution.py:43
  13.1 1.3 collective-permute-start.2
  14.5 0.9 slice.99
  15.4 0.9 collective-permute-done.1
  16.3 1.1 collective-permute-done.2
  17.5 2.2 collective-permute-start.4
  20.2 1.3 collective-permute-start.3
  21.5 4.2 %collective-permute-done.4 = bf16[4,32,1024]{2,1,0:T(8,128)(2,1)S(1)} collective-permute-done((bf16[4,32,1024]{2,1,0:T(8,128)(2,1)S(1)}, bf16[4,32,1024]{2,1,0:T(8,128)(2,1)S(1)}, u32[]{:S(2)}, u32[]{:S(2)}) %collective-permute-start.4) | collective-permute-done | bytes 262176 | tf_op jit(solution)/shard_map/out_weight_columns/ppermute | solution.py:35
  25.8 2.0 collective-permute-start.5
  27.8 3.6 %collective-permute-start.6 = (bf16[2,4,32,1024]{3,2,1,0:T(8,128)(2,1)S(1)}, bf16[2,4,32,1024]{3,2,1,0:T(8,128)(2,1)}, u32[]{:S(2)}, u32[]{:S(2)}) collective-permute-start(bf16[2,4,32,1024]{3,2,1,0:T(8,128)(2,1)S(1)} %pad_maximum_fusion.2), channel_id=1, source_target_pairs={{0,16},{4,20},{8,24},{12,28},{16,0},{20,4},{24,8},{28,12},{32,48},... | collective-permute-start | bytes 1572872 | tf_op jit(solution)/shard_map/out_weight_columns/ppermute | solution.py:31
  31.3 1.0 collective-permute-start.7
  32.3 0.8 fusion.1.one
  33.1 3.8 %collective-permute-done.3 = bf16[256,1024]{1,0:T(8,128)(2,1)S(1)} collective-permute-done((bf16[256,1024]{1,0:T(8,128)(2,1)S(1)}, bf16[256,1024]{1,0:T(8,128)(2,1)S(1)}, u32[]{:S(2)}, u32[]{:S(2)}) %collective-permute-start.3) | collective-permute-done | bytes 524320 | tf_op jit(solution)/shard_map/ppermute | solution.py:335
  37.0 0.9 slice_select_fusion.two
  37.9 3.9 %collective-permute-done.5 = bf16[2,4,32,1024]{3,2,1,0:T(8,128)(2,1)S(1)} collective-permute-done((bf16[2,4,32,1024]{3,2,1,0:T(8,128)(2,1)S(1)}, bf16[2,4,32,1024]{3,2,1,0:T(8,128)(2,1)S(1)}, u32[]{:S(2)}, u32[]{:S(2)}) %collective-permute-start.5) | collective-permute-done | bytes 524320 | tf_op jit(solution)/shard_map/out_weight_columns/ppermute | solution.py:31
  41.8 10.2 %collective-permute-done.6 = bf16[2,4,32,1024]{3,2,1,0:T(8,128)(2,1)} collective-permute-done((bf16[2,4,32,1024]{3,2,1,0:T(8,128)(2,1)S(1)}, bf16[2,4,32,1024]{3,2,1,0:T(8,128)(2,1)}, u32[]{:S(2)}, u32[]{:S(2)}) %collective-permute-start.6) | collective-permute-done | bytes 524320 | tf_op jit(solution)/shard_map/out_weight_columns/ppermute | solution.py:31
  52.0 7.6 %products.1 = (bf16[128,4096]{1,0:T(8,128)(2,1)}, bf16[256,4096]{1,0:T(8,128)(2,1)}) custom-call(bf16[128,1024]{1,0:T(8,128)(2,1)} %fusion.1.one, bf16[256,1024]{1,0:T(8,128)(2,1)} %slice_select_fusion.two, bf16[1024,4096]{1,0:T(8,128)(2,1)} %right.1), custom_call_target="tpu_custom_call" | custom-call | flops 3221225472 | bytes 1048576 | tf_op jit(solution)/shard_map/products/pallas_call | solution.py:140
  59.6 0.7 reduce-scatter.3.cloned.1.call-update
  61.2 13.8 %qkv.1 = bf16[4,3,512,128]{3,2,1,0:T(8,128)(2,1)} custom-call(s32[5]{0:T(128)} %stack.97.place, bf16[512,4096]{1,0:T(8,128)(2,1)} %bitcast.89, f32[4,4096]{1,0:T(4,128)} %bitcast.87, bf16[3,4096,512]{2,1,0:T(8,128)(2,1)} %bitcast.88, bf16[128,4096]{1,0:T(8,128)(2,1)} %get-tuple-element.18.rest_0_, bf16[256,4096]{1,0:T(8,128)(2,1)} %get-tuple-element.19.rest_1_), custom_call_target="tpu_custom_call" | custom-call | flops 6442450944 | bytes 1048576 | tf_op jit(solution)/shard_map/qkv/pallas_call | solution.py:114
  75.0 1.3 slice_bitcast_fusion.2
  76.4 1.3 collective-permute-start.8
  77.7 2.4 %collective-permute-start.9 = (bf16[3,512,128]{2,1,0:T(8,128)(2,1)S(1)}, bf16[3,512,128]{2,1,0:T(8,128)(2,1)S(1)}, u32[]{:S(2)}, u32[]{:S(2)}) collective-permute-start(bf16[3,512,128]{2,1,0:T(8,128)(2,1)S(1)} %get-tuple-element.35), channel_id=1, source_target_pairs={{0,16},{4,20},{8,24},{12,28},{16,0},{20,4},{24,8},{28,12},{32,48},... | collective-permute-start | bytes 1179656 | tf_op jit(solution)/shard_map/ppermute | solution.py:31
  80.0 1.3 collective-permute-start.10
  81.3 1.0 slice_bitcast_fusion.3
  82.3 5.6 %collective-permute-done.8 = bf16[3,512,128]{2,1,0:T(8,128)(2,1)S(1)} collective-permute-done((bf16[3,512,128]{2,1,0:T(8,128)(2,1)S(1)}, bf16[3,512,128]{2,1,0:T(8,128)(2,1)S(1)}, u32[]{:S(2)}, u32[]{:S(2)}) %collective-permute-start.8) | collective-permute-done | bytes 393248 | tf_op jit(solution)/shard_map/ppermute | solution.py:31
  87.9 9.6 %collective-permute-done.9 = bf16[3,512,128]{2,1,0:T(8,128)(2,1)S(1)} collective-permute-done((bf16[3,512,128]{2,1,0:T(8,128)(2,1)S(1)}, bf16[3,512,128]{2,1,0:T(8,128)(2,1)S(1)}, u32[]{:S(2)}, u32[]{:S(2)}) %collective-permute-start.9) | collective-permute-done | bytes 393248 | tf_op jit(solution)/shard_map/ppermute | solution.py:31
  97.5 0.7 copy-done.15
  98.2 0.8 copy-done.16
  99.2 1.8 pad_maximum_fusion
  101.5 1.0 slice_bitcast_fusion.7
  102.6 2.4 %collective-permute-start.11 = (bf16[2,2048,128]{2,1,0:T(8,128)(2,1)S(1)}, bf16[2,2048,128]{2,1,0:T(8,128)(2,1)}, u32[]{:S(2)}, u32[]{:S(2)}) collective-permute-start(bf16[2,2048,128]{2,1,0:T(8,128)(2,1)S(1)} %pad_maximum_fusion.1.refs_1_), channel_id=1, source_target_pairs={{0,32},{4,36},{8,40},{12,44},{16,48},{20,52},{24,56},{28,60},{32,0... | collective-permute-start | bytes 3145736 | tf_op jit(solution)/shard_map/ppermute | solution.py:35
  105.0 0.9 slice_bitcast_fusion.4
  105.9 0.9 slice_bitcast_fusion.5
  106.9 0.8 pad_maximum_fusion.3.refs_0_
  107.7 1.0 copy-done.17
  108.7 1.3 copy-done.5
  110.0 13.9 %attention.2 = (f32[2048,128]{1,0:T(8,128)}, f32[2048,128]{1,0:T(8,128)}, f32[2048,128]{1,0:T(8,128)}) custom-call(bf16[2048,128]{1,0:T(8,128)(2,1)} %pad_maximum_fusion.3.refs_0_, bf16[2,2048,128]{2,1,0:T(8,128)(2,1)} %copy-done.12, bf16[2,2048,128]{2,1,0:T(8,128)(2,1)} %copy-done.17, bf16[8,4,32,1024]{3,2,1,0:T(8,128)(2,1)} %bitcast.75, ...), custom_call_target="tpu_custom_call" | custom-call | flops 4294967296 | bytes 2097152 | tf_op jit(solution)/shard_map/attention/pallas_call | solution.py:210
  123.9 5.7 %collective-permute-done.11.refs_1_ = bf16[2,2048,128]{2,1,0:T(8,128)(2,1)} collective-permute-done((bf16[2,2048,128]{2,1,0:T(8,128)(2,1)S(1)}, bf16[2,2048,128]{2,1,0:T(8,128)(2,1)}, u32[]{:S(2)}, u32[]{:S(2)}) %collective-permute-start.11) | collective-permute-done | bytes 1048608 | tf_op jit(solution)/shard_map/ppermute | solution.py:35
  129.6 2.9 %collective-permute-done.14.refs_2_ = bf16[2,2048,128]{2,1,0:T(8,128)(2,1)S(1)} collective-permute-done((bf16[2,2048,128]{2,1,0:T(8,128)(2,1)}, bf16[2,2048,128]{2,1,0:T(8,128)(2,1)S(1)}, u32[]{:S(2)}, u32[]{:S(2)}) %collective-permute-start.14) | collective-permute-done | bytes 1048608 | tf_op jit(solution)/shard_map/ppermute | solution.py:39
  132.4 1.0 copy-done.18
  133.4 14.1 %attention.3 = bf16[2048,128]{1,0:T(8,128)(2,1)} custom-call(bf16[2048,128]{1,0:T(8,128)(2,1)} %pad_maximum_fusion.3.refs_0_, bf16[2,2048,128]{2,1,0:T(8,128)(2,1)} %collective-permute-done.11.refs_1_, bf16[2,2048,128]{2,1,0:T(8,128)(2,1)} %copy-done.18, bf16[256,1024]{1,0:T(8,128)(2,1)} %reduce-scatter.3.cloned.1.call-done.refs_3_.refs_13_.refs_6_, ...), custom_call_target="tpu_custom_call" | custom-call | flops 4294967296 | bytes 2097152 | tf_op jit(solution)/shard_map/attention/pallas_call | solution.py:210
  147.5 1.1 fusion.3
  148.5 1.5 collective-permute-start.15
  150.0 0.9 collective-permute-start.16
  151.0 0.9 slice_bitcast_fusion.11
  151.9 4.1 %collective-permute-done.15 = bf16[512,128]{1,0:T(8,128)(2,1)S(1)} collective-permute-done((bf16[512,128]{1,0:T(8,128)(2,1)S(1)}, bf16[512,128]{1,0:T(8,128)(2,1)S(1)}, u32[]{:S(2)}, u32[]{:S(2)}) %collective-permute-start.15) | collective-permute-done | bytes 131104 | tf_op jit(solution)/shard_map/ppermute | solution.py:31
  156.0 4.2 %collective-permute-done.16 = bf16[512,128]{1,0:T(8,128)(2,1)S(1)} collective-permute-done((bf16[512,128]{1,0:T(8,128)(2,1)S(1)}, bf16[512,128]{1,0:T(8,128)(2,1)S(1)}, u32[]{:S(2)}, u32[]{:S(2)}) %collective-permute-start.16) | collective-permute-done | bytes 131104 | tf_op jit(solution)/shard_map/ppermute | solution.py:31
  160.2 2.3 %collective-permute-done.17 = bf16[512,128]{1,0:T(8,128)(2,1)S(1)} collective-permute-done((bf16[512,128]{1,0:T(8,128)(2,1)S(1)}, bf16[512,128]{1,0:T(8,128)(2,1)S(1)}, u32[]{:S(2)}, u32[]{:S(2)}) %collective-permute-start.17) | collective-permute-done | bytes 131104 | tf_op jit(solution)/shard_map/ppermute | solution.py:31
  162.6 3.2 %collective-permute-start.19 = (bf16[4,256,128]{2,1,0:T(8,128)(2,1)S(1)}, bf16[4,256,128]{2,1,0:T(8,128)(2,1)S(1)}, u32[]{:S(2)}, u32[]{:S(2)}) collective-permute-start(bf16[4,256,128]{2,1,0:T(8,128)(2,1)S(1)} %pad_maximum_fusion.6.refs_0_), channel_id=1, source_target_pairs={{0,2},{1,3},{2,0},{3,1},{4,6},{5,7},{6,4},{7,5},{8,10},{9,11},{10,... | collective-permute-start | bytes 786440 | tf_op jit(solution)/shard_map/ppermute | solution.py:43
  166.4 1.5 collective-permute-start.21
  167.9 1.0 collective-permute-start.22
  168.9 9.6 %collective-permute-done.18.refs_1_ = bf16[4,256,128]{2,1,0:T(8,128)(2,1)S(1)} collective-permute-done((bf16[4,256,128]{2,1,0:T(8,128)(2,1)S(1)}, bf16[4,256,128]{2,1,0:T(8,128)(2,1)S(1)}, u32[]{:S(2)}, u32[]{:S(2)}) %collective-permute-start.18) | collective-permute-done | bytes 262176 | tf_op jit(solution)/shard_map/ppermute | solution.py:43
  180.2 5.6 %residual.2 = bf16[256,1024]{1,0:T(8,128)(2,1)} custom-call(s32[5]{0:T(128)} %stack.97.place, bf16[4,256,128]{2,1,0:T(8,128)(2,1)} %copy-done.3, bf16[4,256,128]{2,1,0:T(8,128)(2,1)} %copy-done.6, bf16[4,256,128]{2,1,0:T(8,128)(2,1)} %copy-done.7, bf16[4,256,128]{2,1,0:T(8,128)(2,1)} %copy-done.8, ...), custom_call_target="tpu_custom_call" | custom-call | flops 1073741824 | bytes 1048576 | tf_op jit(solution)/shard_map/residual/pallas_call | solution.py:283
  185.9 1.3 collective-permute-start.24
  187.2 1.6 collective-permute-done.22.refs_6_.refs_2_
  189.5 0.7 copy-done.11
  190.2 5.4 %residual.3 = bf16[256,1024]{1,0:T(8,128)(2,1)} custom-call(s32[5]{0:T(128)} %stack.97.place, bf16[4,256,128]{2,1,0:T(8,128)(2,1)} %copy-done.4, bf16[4,256,128]{2,1,0:T(8,128)(2,1)} %copy-done.9, bf16[4,256,128]{2,1,0:T(8,128)(2,1)} %copy-done.10, bf16[4,256,128]{2,1,0:T(8,128)(2,1)} %copy-done.11, ...), custom_call_target="tpu_custom_call" | custom-call | flops 1073741824 | bytes 1048576 | tf_op jit(solution)/shard_map/residual/pallas_call | solution.py:283
  195.7 1.3 collective-permute-start.25
  197.0 8.3 %blended.1 = f32[512,1024]{1,0:T(8,128)} custom-call(s32[5]{0:T(128)} %stack.97.place, bf16[4,256,128]{2,1,0:T(8,128)(2,1)} %copy-done.3, bf16[4,256,128]{2,1,0:T(8,128)(2,1)} %copy-done.6, bf16[4,256,128]{2,1,0:T(8,128)(2,1)} %copy-done.7, bf16[4,256,128]{2,1,0:T(8,128)(2,1)} %copy-done.8, bf16[4,256,128]{2,1,0:T(8,128)(2,1)} %copy-done.4, ...), custom_call_target="tpu_custom_call" | custom-call | flops 2147483648 | bytes 1048576 | tf_op jit(solution)/shard_map/blended/pallas_call | solution.py:283
  205.3 6.1 %collective-permute-done.25 = bf16[256,1024]{1,0:T(8,128)(2,1)S(1)} collective-permute-done((bf16[256,1024]{1,0:T(8,128)(2,1)}, bf16[256,1024]{1,0:T(8,128)(2,1)S(1)}, u32[]{:S(2)}, u32[]{:S(2)}) %collective-permute-start.25) | collective-permute-done | bytes 524320 | tf_op jit(solution)/shard_map/ppermute | solution.py:370
  211.4 2.9 %fusion = bf16[1,512,1024]{2,1,0:T(8,128)(2,1)} fusion(f32[512,1024]{1,0:T(8,128)} %blended.1, bf16[256,1024]{1,0:T(8,128)(2,1)S(1)} %collective-permute-done.25, bf16[256,1024]{1,0:T(8,128)(2,1)S(1)} %collective-permute-done.24), kind=kLoop, calls=%fused_computation.3 | loop fusion | flops 3145728 | bytes 4194304 | tf_op jit(solution)/shard_map/broadcast_in_dim | solution.py:374
  (78 shorter events, 5.6 us)
Async XLA Ops:
  6.5 13.2 %copy-start = (bf16[1,512,1024]{2,1,0:T(8,128)(2,1)S(1)}, bf16[1,512,1024]{2,1,0:T(8,128)(2,1)}, u32[]{:S(2)}) copy-start(bf16[1,512,1024]{2,1,0:T(8,128)(2,1)} %param.6) | copy-start | bytes 3145732
  6.5 13.2 %copy-start.2 = (bf16[1,512,1024]{2,1,0:T(8,128)(2,1)S(1)}, bf16[1,512,1024]{2,1,0:T(8,128)(2,1)}, u32[]{:S(2)}) copy-start(bf16[1,512,1024]{2,1,0:T(8,128)(2,1)} %param.11) | copy-start | bytes 3145732
  6.5 54.7 %all-gather.6.cloned.1.call-start = ((), (), s32[]{:S(2)}) async-start(), calls=%async_computation.5 | async-start | bytes 5242880 | tf_op jit(solution)/shard_map/all_gather | solution.py:323
  7.3 91.9 %reduce-scatter.5.cloned.1.call-start = ((), (), s32[]{:S(2)}) async-start(), calls=%async_computation.3 | async-start | bytes 1310720 | tf_op jit(solution)/shard_map/reduce_scatter | solution.py:339
  8.6 6.9 %collective-permute-start = (bf16[32,1024]{1,0:T(8,128)(2,1)S(1)}, bf16[32,1024]{1,0:T(8,128)(2,1)S(1)}, u32[]{:S(2)}, u32[]{:S(2)}) collective-permute-start(bf16[32,1024]{1,0:T(8,128)(2,1)S(1)} %get-tuple-element.30), channel_id=1, source_target_pairs={{0,1},{1,2},{2,3},{3,0},{4,5},{5,6},{6,7},{7,4},{8,9},{9,10},{10,1... | collective-permute-start | bytes 196616 | tf_op jit(solution)/shard_map/out_weight_columns/ppermute | solution.py:43
  10.2 6.1 %collective-permute-start.1 = (bf16[32,1024]{1,0:T(8,128)(2,1)S(1)}, bf16[32,1024]{1,0:T(8,128)(2,1)S(1)}, u32[]{:S(2)}, u32[]{:S(2)}) collective-permute-start(bf16[32,1024]{1,0:T(8,128)(2,1)S(1)} %get-tuple-element.32), channel_id=1, source_target_pairs={{0,2},{1,3},{2,0},{3,1},{4,6},{5,7},{6,4},{7,5},{8,10},{9,11},{10,... | collective-permute-start | bytes 196616 | tf_op jit(solution)/shard_map/out_weight_columns/ppermute | solution.py:43
  13.1 4.3 %collective-permute-start.2 = (bf16[32,1024]{1,0:T(8,128)(2,1)S(1)}, bf16[32,1024]{1,0:T(8,128)(2,1)S(1)}, u32[]{:S(2)}, u32[]{:S(2)}) collective-permute-start(bf16[32,1024]{1,0:T(8,128)(2,1)S(1)} %get-tuple-element.31), channel_id=1, source_target_pairs={{0,3},{1,0},{2,1},{3,2},{4,7},{5,4},{6,5},{7,6},{8,11},{9,8},{10,9... | collective-permute-start | bytes 196616 | tf_op jit(solution)/shard_map/out_weight_columns/ppermute | solution.py:43
  17.5 8.2 %collective-permute-start.4 = (bf16[4,32,1024]{2,1,0:T(8,128)(2,1)S(1)}, bf16[4,32,1024]{2,1,0:T(8,128)(2,1)S(1)}, u32[]{:S(2)}, u32[]{:S(2)}) collective-permute-start(bf16[4,32,1024]{2,1,0:T(8,128)(2,1)S(1)} %get-tuple-element.42), channel_id=1, source_target_pairs={{0,32},{4,36},{8,40},{12,44},{16,48},{20,52},{24,56},{28,60},{32,0... | collective-permute-start | bytes 786440 | tf_op jit(solution)/shard_map/out_weight_columns/ppermute | solution.py:35
  20.2 16.8 %collective-permute-start.3 = (bf16[256,1024]{1,0:T(8,128)(2,1)S(1)}, bf16[256,1024]{1,0:T(8,128)(2,1)S(1)}, u32[]{:S(2)}, u32[]{:S(2)}) collective-permute-start(bf16[256,1024]{1,0:T(8,128)(2,1)S(1)} %slice.128), channel_id=1, source_target_pairs={{0,64},{1,65},{2,66},{3,67},{4,68},{5,69},{6,70},{7,71},{8,72},{9,... | collective-permute-start | bytes 1572872 | tf_op jit(solution)/shard_map/ppermute | solution.py:335
  25.8 16.0 %collective-permute-start.5 = (bf16[2,4,32,1024]{3,2,1,0:T(8,128)(2,1)S(1)}, bf16[2,4,32,1024]{3,2,1,0:T(8,128)(2,1)S(1)}, u32[]{:S(2)}, u32[]{:S(2)}) collective-permute-start(bf16[2,4,32,1024]{3,2,1,0:T(8,128)(2,1)S(1)} %pad_maximum_fusion.2), channel_id=1, source_target_pairs={{0,8},{4,12},{8,16},{12,20},{16,24},{20,28},{24,0},{28,4},{32,40},... | collective-permute-start | bytes 1572872 | tf_op jit(solution)/shard_map/out_weight_columns/ppermute | solution.py:31
  27.8 24.2 %collective-permute-start.6 = (bf16[2,4,32,1024]{3,2,1,0:T(8,128)(2,1)S(1)}, bf16[2,4,32,1024]{3,2,1,0:T(8,128)(2,1)}, u32[]{:S(2)}, u32[]{:S(2)}) collective-permute-start(bf16[2,4,32,1024]{3,2,1,0:T(8,128)(2,1)S(1)} %pad_maximum_fusion.2), channel_id=1, source_target_pairs={{0,16},{4,20},{8,24},{12,28},{16,0},{20,4},{24,8},{28,12},{32,48},... | collective-permute-start | bytes 1572872 | tf_op jit(solution)/shard_map/out_weight_columns/ppermute | solution.py:31
  31.3 20.6 %collective-permute-start.7 = (bf16[2,4,32,1024]{3,2,1,0:T(8,128)(2,1)S(1)}, bf16[2,4,32,1024]{3,2,1,0:T(8,128)(2,1)}, u32[]{:S(2)}, u32[]{:S(2)}) collective-permute-start(bf16[2,4,32,1024]{3,2,1,0:T(8,128)(2,1)S(1)} %pad_maximum_fusion.2), channel_id=1, source_target_pairs={{0,24},{4,28},{8,0},{12,4},{16,8},{20,12},{24,16},{28,20},{32,56},... | collective-permute-start | bytes 1572872 | tf_op jit(solution)/shard_map/out_weight_columns/ppermute | solution.py:31
  41.8 17.7 %copy-start.13 = (bf16[2,4,32,1024]{3,2,1,0:T(8,128)(2,1)}, bf16[2,4,32,1024]{3,2,1,0:T(8,128)(2,1)S(1)}, u32[]{:S(2)}) copy-start(bf16[2,4,32,1024]{3,2,1,0:T(8,128)(2,1)S(1)} %collective-permute-done.5) | copy-start | bytes 1572868
  59.6 70.0 %reduce-scatter.3.cloned.1.call-start = ((), (), s32[]{:S(2)}) async-start(), calls=%async_computation.2 | async-start | bytes 2621440 | tf_op jit(solution)/shard_map/early_residual/reduce_scatter | solution.py:343
  60.3 119.2 %all-gather.4.cloned.1.call-start = ((), (), s32[]{:S(2)}) async-start(), calls=%async_computation.4 | async-start | bytes 4456448 | tf_op jit(solution)/shard_map/joint_weight/all_gather | solution.py:357
  76.4 11.5 %collective-permute-start.8 = (bf16[3,512,128]{2,1,0:T(8,128)(2,1)S(1)}, bf16[3,512,128]{2,1,0:T(8,128)(2,1)S(1)}, u32[]{:S(2)}, u32[]{:S(2)}) collective-permute-start(bf16[3,512,128]{2,1,0:T(8,128)(2,1)S(1)} %get-tuple-element.33), channel_id=1, source_target_pairs={{0,8},{4,12},{8,16},{12,20},{16,24},{20,28},{24,0},{28,4},{32,40},... | collective-permute-start | bytes 1179656 | tf_op jit(solution)/shard_map/ppermute | solution.py:31
  77.7 19.8 %collective-permute-start.9 = (bf16[3,512,128]{2,1,0:T(8,128)(2,1)S(1)}, bf16[3,512,128]{2,1,0:T(8,128)(2,1)S(1)}, u32[]{:S(2)}, u32[]{:S(2)}) collective-permute-start(bf16[3,512,128]{2,1,0:T(8,128)(2,1)S(1)} %get-tuple-element.35), channel_id=1, source_target_pairs={{0,16},{4,20},{8,24},{12,28},{16,0},{20,4},{24,8},{28,12},{32,48},... | collective-permute-start | bytes 1179656 | tf_op jit(solution)/shard_map/ppermute | solution.py:31
  80.0 17.5 %collective-permute-start.10 = (bf16[3,512,128]{2,1,0:T(8,128)(2,1)S(1)}, bf16[3,512,128]{2,1,0:T(8,128)(2,1)S(1)}, u32[]{:S(2)}, u32[]{:S(2)}) collective-permute-start(bf16[3,512,128]{2,1,0:T(8,128)(2,1)S(1)} %get-tuple-element.34), channel_id=1, source_target_pairs={{0,24},{4,28},{8,0},{12,4},{16,8},{20,12},{24,16},{28,20},{32,56},... | collective-permute-start | bytes 1179656 | tf_op jit(solution)/shard_map/ppermute | solution.py:31
  82.3 16.9 %copy-start.14 = (bf16[2,4,32,1024]{3,2,1,0:T(8,128)(2,1)S(1)}, bf16[2,4,32,1024]{3,2,1,0:T(8,128)(2,1)}, u32[]{:S(2)}) copy-start(bf16[2,4,32,1024]{3,2,1,0:T(8,128)(2,1)} %copy-done.13) | copy-start | bytes 1572868
  97.5 0.7 copy-start.15
  98.2 0.8 copy-start.16
  99.1 3.5 %copy-start.12 = (bf16[2,2048,128]{2,1,0:T(8,128)(2,1)}, bf16[2,2048,128]{2,1,0:T(8,128)(2,1)S(1)}, u32[]{:S(2)}) copy-start(bf16[2,2048,128]{2,1,0:T(8,128)(2,1)S(1)} %pad_maximum_fusion.1.refs_1_) | copy-start | bytes 3145732
  100.9 7.7 %copy-start.1 = (bf16[4,2,4,32,1024]{4,3,2,1,0:T(8,128)(2,1)}, bf16[4,2,4,32,1024]{4,3,2,1,0:T(8,128)(2,1)S(1)}, u32[]{:S(2)}) copy-start(bf16[4,2,4,32,1024]{4,3,2,1,0:T(8,128)(2,1)S(1)} %pad_maximum_fusion) | copy-start | bytes 6291460
  101.0 7.7 %collective-permute-start.13 = (bf16[8,4,32,1024]{3,2,1,0:T(8,128)(2,1)S(1)}, bf16[8,4,32,1024]{3,2,1,0:T(8,128)(2,1)S(1)}, u32[]{:S(2)}, u32[]{:S(2)}) collective-permute-start(bf16[8,4,32,1024]{3,2,1,0:T(8,128)(2,1)S(1)} %bitcast.74), channel_id=1, source_target_pairs={{0,4},{4,0},{8,12},{12,8},{16,20},{20,16},{24,28},{28,24},{32,36},... | collective-permute-start | bytes 6291464 | tf_op jit(solution)/shard_map/out_weight_columns/ppermute | solution.py:39
  101.1 6.7 %collective-permute-start.12 = (bf16[2,2048,128]{2,1,0:T(8,128)(2,1)S(1)}, bf16[2,2048,128]{2,1,0:T(8,128)(2,1)S(1)}, u32[]{:S(2)}, u32[]{:S(2)}) collective-permute-start(bf16[2,2048,128]{2,1,0:T(8,128)(2,1)S(1)} %pad_maximum_fusion.1.refs_1_), channel_id=1, source_target_pairs={{0,4},{4,0},{8,12},{12,8},{16,20},{20,16},{24,28},{28,24},{32,36},... | collective-permute-start | bytes 3145736 | tf_op jit(solution)/shard_map/ppermute | solution.py:39
  102.6 26.9 %collective-permute-start.11 = (bf16[2,2048,128]{2,1,0:T(8,128)(2,1)S(1)}, bf16[2,2048,128]{2,1,0:T(8,128)(2,1)}, u32[]{:S(2)}, u32[]{:S(2)}) collective-permute-start(bf16[2,2048,128]{2,1,0:T(8,128)(2,1)S(1)} %pad_maximum_fusion.1.refs_1_), channel_id=1, source_target_pairs={{0,32},{4,36},{8,40},{12,44},{16,48},{20,52},{24,56},{28,60},{32,0... | collective-permute-start | bytes 3145736 | tf_op jit(solution)/shard_map/ppermute | solution.py:35
  107.7 1.0 copy-start.17
  108.7 1.3 copy-start.5
  129.5 2.9 %collective-permute-start.14 = (bf16[2,2048,128]{2,1,0:T(8,128)(2,1)}, bf16[2,2048,128]{2,1,0:T(8,128)(2,1)S(1)}, u32[]{:S(2)}, u32[]{:S(2)}) collective-permute-start(bf16[2,2048,128]{2,1,0:T(8,128)(2,1)} %collective-permute-done.11.refs_1_), channel_id=1, source_target_pairs={{0,4},{4,0},{8,12},{12,8},{16,20},{20,16},{24,28},{28,24},{32,36},... | collective-permute-start | bytes 3145736 | tf_op jit(solution)/shard_map/ppermute | solution.py:39
  132.4 1.0 copy-start.18
  148.5 7.5 %collective-permute-start.15 = (bf16[512,128]{1,0:T(8,128)(2,1)S(1)}, bf16[512,128]{1,0:T(8,128)(2,1)S(1)}, u32[]{:S(2)}, u32[]{:S(2)}) collective-permute-start(bf16[512,128]{1,0:T(8,128)(2,1)S(1)} %get-tuple-element.38), channel_id=1, source_target_pairs={{0,24},{4,28},{8,0},{12,4},{16,8},{20,12},{24,16},{28,20},{32,56},... | collective-permute-start | bytes 393224 | tf_op jit(solution)/shard_map/ppermute | solution.py:31
  150.0 10.1 %collective-permute-start.16 = (bf16[512,128]{1,0:T(8,128)(2,1)S(1)}, bf16[512,128]{1,0:T(8,128)(2,1)S(1)}, u32[]{:S(2)}, u32[]{:S(2)}) collective-permute-start(bf16[512,128]{1,0:T(8,128)(2,1)S(1)} %get-tuple-element.40), channel_id=1, source_target_pairs={{0,16},{4,20},{8,24},{12,28},{16,0},{20,4},{24,8},{28,12},{32,48},... | collective-permute-start | bytes 393224 | tf_op jit(solution)/shard_map/ppermute | solution.py:31
  151.0 11.4 %collective-permute-start.17 = (bf16[512,128]{1,0:T(8,128)(2,1)S(1)}, bf16[512,128]{1,0:T(8,128)(2,1)S(1)}, u32[]{:S(2)}, u32[]{:S(2)}) collective-permute-start(bf16[512,128]{1,0:T(8,128)(2,1)S(1)} %get-tuple-element.39), channel_id=1, source_target_pairs={{0,8},{4,12},{8,16},{12,20},{16,24},{20,28},{24,0},{28,4},{32,40},... | collective-permute-start | bytes 393224 | tf_op jit(solution)/shard_map/ppermute | solution.py:31
  162.5 17.0 %copy-start.3 = (bf16[4,256,128]{2,1,0:T(8,128)(2,1)}, bf16[4,256,128]{2,1,0:T(8,128)(2,1)S(1)}, u32[]{:S(2)}) copy-start(bf16[4,256,128]{2,1,0:T(8,128)(2,1)S(1)} %pad_maximum_fusion.6.refs_0_) | copy-start | bytes 786436
  162.5 16.1 %collective-permute-start.18 = (bf16[4,256,128]{2,1,0:T(8,128)(2,1)S(1)}, bf16[4,256,128]{2,1,0:T(8,128)(2,1)S(1)}, u32[]{:S(2)}, u32[]{:S(2)}) collective-permute-start(bf16[4,256,128]{2,1,0:T(8,128)(2,1)S(1)} %pad_maximum_fusion.6.refs_0_), channel_id=1, source_target_pairs={{0,1},{1,2},{2,3},{3,0},{4,5},{5,6},{6,7},{7,4},{8,9},{9,10},{10,1... | collective-permute-start | bytes 786440 | tf_op jit(solution)/shard_map/ppermute | solution.py:43
  162.6 16.6 %collective-permute-start.19 = (bf16[4,256,128]{2,1,0:T(8,128)(2,1)S(1)}, bf16[4,256,128]{2,1,0:T(8,128)(2,1)S(1)}, u32[]{:S(2)}, u32[]{:S(2)}) collective-permute-start(bf16[4,256,128]{2,1,0:T(8,128)(2,1)S(1)} %pad_maximum_fusion.6.refs_0_), channel_id=1, source_target_pairs={{0,2},{1,3},{2,0},{3,1},{4,6},{5,7},{6,4},{7,5},{8,10},{9,11},{10,... | collective-permute-start | bytes 786440 | tf_op jit(solution)/shard_map/ppermute | solution.py:43
  165.8 13.7 %collective-permute-start.20 = (bf16[4,256,128]{2,1,0:T(8,128)(2,1)S(1)}, bf16[4,256,128]{2,1,0:T(8,128)(2,1)S(1)}, u32[]{:S(2)}, u32[]{:S(2)}) collective-permute-start(bf16[4,256,128]{2,1,0:T(8,128)(2,1)S(1)} %pad_maximum_fusion.6.refs_0_), channel_id=1, source_target_pairs={{0,3},{1,0},{2,1},{3,2},{4,7},{5,4},{6,5},{7,6},{8,11},{9,8},{10,9... | collective-permute-start | bytes 786440 | tf_op jit(solution)/shard_map/ppermute | solution.py:43
  166.4 19.4 %copy-start.4 = (bf16[4,256,128]{2,1,0:T(8,128)(2,1)}, bf16[4,256,128]{2,1,0:T(8,128)(2,1)S(1)}, u32[]{:S(2)}) copy-start(bf16[4,256,128]{2,1,0:T(8,128)(2,1)S(1)} %pad_maximum_fusion.7.refs_4_.refs_0_) | copy-start | bytes 786436
  166.4 20.7 %collective-permute-start.21 = (bf16[4,256,128]{2,1,0:T(8,128)(2,1)S(1)}, bf16[4,256,128]{2,1,0:T(8,128)(2,1)S(1)}, u32[]{:S(2)}, u32[]{:S(2)}) collective-permute-start(bf16[4,256,128]{2,1,0:T(8,128)(2,1)S(1)} %pad_maximum_fusion.7.refs_4_.refs_0_), channel_id=1, source_target_pairs={{0,1},{1,2},{2,3},{3,0},{4,5},{5,6},{6,7},{7,4},{8,9},{9,10},{10,1... | collective-permute-start | bytes 786440 | tf_op jit(solution)/shard_map/ppermute | solution.py:43
  167.9 20.9 %collective-permute-start.22 = (bf16[4,256,128]{2,1,0:T(8,128)(2,1)S(1)}, bf16[4,256,128]{2,1,0:T(8,128)(2,1)S(1)}, u32[]{:S(2)}, u32[]{:S(2)}) collective-permute-start(bf16[4,256,128]{2,1,0:T(8,128)(2,1)S(1)} %pad_maximum_fusion.7.refs_4_.refs_0_), channel_id=1, source_target_pairs={{0,2},{1,3},{2,0},{3,1},{4,6},{5,7},{6,4},{7,5},{8,10},{9,11},{10,... | collective-permute-start | bytes 786440 | tf_op jit(solution)/shard_map/ppermute | solution.py:43
  178.5 1.0 copy-start.6
  178.5 10.9 %collective-permute-start.23 = (bf16[4,256,128]{2,1,0:T(8,128)(2,1)S(1)}, bf16[4,256,128]{2,1,0:T(8,128)(2,1)S(1)}, u32[]{:S(2)}, u32[]{:S(2)}) collective-permute-start(bf16[4,256,128]{2,1,0:T(8,128)(2,1)S(1)} %pad_maximum_fusion.7.refs_4_.refs_0_), channel_id=1, source_target_pairs={{0,3},{1,0},{2,1},{3,2},{4,7},{5,4},{6,5},{7,6},{8,11},{9,8},{10,9... | collective-permute-start | bytes 786440 | tf_op jit(solution)/shard_map/ppermute | solution.py:43
  179.2 0.7 copy-start.7
  179.5 0.7 copy-start.8
  185.9 19.4 %collective-permute-start.24 = (bf16[256,1024]{1,0:T(8,128)(2,1)}, bf16[256,1024]{1,0:T(8,128)(2,1)S(1)}, u32[]{:S(2)}, u32[]{:S(2)}) collective-permute-start(bf16[256,1024]{1,0:T(8,128)(2,1)} %residual.2), channel_id=1, source_target_pairs={{0,64},{1,65},{2,66},{3,67},{4,68},{5,69},{6,70},{7,71},{8,72},{9,... | collective-permute-start | bytes 1572872 | tf_op jit(solution)/shard_map/ppermute | solution.py:370
  187.2 2.2 %copy-start.9 = (bf16[4,256,128]{2,1,0:T(8,128)(2,1)}, bf16[4,256,128]{2,1,0:T(8,128)(2,1)S(1)}, u32[]{:S(2)}) copy-start(bf16[4,256,128]{2,1,0:T(8,128)(2,1)S(1)} %collective-permute-done.21.refs_5_.refs_1_) | copy-start | bytes 786436
  188.8 0.7 copy-start.10
  189.5 0.7 copy-start.11
  195.7 15.7 %collective-permute-start.25 = (bf16[256,1024]{1,0:T(8,128)(2,1)}, bf16[256,1024]{1,0:T(8,128)(2,1)S(1)}, u32[]{:S(2)}, u32[]{:S(2)}) collective-permute-start(bf16[256,1024]{1,0:T(8,128)(2,1)} %residual.3), channel_id=1, source_target_pairs={{0,64},{1,65},{2,66},{3,67},{4,68},{5,69},{6,70},{7,71},{8,72},{9,... | collective-permute-start | bytes 1572872 | tf_op jit(solution)/shard_map/ppermute | solution.py:370
Sparse Core Ops, SparseCore 0:
  9.0 50.6 all-gather.5
  62.1 23.8 reduce-scatter.4
  88.5 29.3 reduce-scatter.2
  120.3 54.2 all-gather.3

commit v3 on v2

--- a/solution.py
+++ b/solution.py
@@ -151,9 +151,16 @@
 
 
 def attention_kernel(*refs, count, gates, first, last):
-    query = refs[0][...]
-    pairs = refs[1 : 1 + count]
-    rest = refs[1 + count + gates :]
+    refs, held = refs[:-1], refs[-1]
+    for index in range(4):
+
+        @pl.when(pl.program_id(0) == index)
+        def _(index=index):
+            held[...] = refs[index][0]
+
+    query = held[...]
+    pairs = refs[4 : 4 + count]
+    rest = refs[4 + count + gates :]
     rows = query.shape[0]
     pieces = []
     for pair in pairs:
@@ -195,13 +202,11 @@
         rest[2][...] = jnp.broadcast_to(total, (rows, HEAD_DIM))
 
 
-def attention(query, pairs, carry, last, part, parts, earlier=()):
-    rows = query.shape[0] // parts
-    block = 512
-    first = part * (rows // block)
+def attention(turned, pairs, carry, last, earlier=()):
+    block = turned[0].shape[1]
+    rows = 4 * block
     tokens = sum(pair.shape[1] for pair in pairs)
     row_block = pl.BlockSpec((block, HEAD_DIM), lambda i: (i, 0))
-    in_block = pl.BlockSpec((block, HEAD_DIM), lambda i: (first + i, 0))
     shape = lambda dtype: jax.ShapeDtypeStruct((rows, HEAD_DIM), dtype)
     if last:
         out_shape, out_specs = shape(jnp.bfloat16), row_block
@@ -210,11 +215,12 @@
     return pl.pallas_call(
         functools.partial(attention_kernel, count=len(pairs), gates=len(earlier), first=not carry, last=last),
         grid=(rows // block,),
-        in_specs=[in_block]
+        in_specs=[pl.BlockSpec((1, block, HEAD_DIM), lambda i: (0, 0, 0))] * 4
         + [pl.BlockSpec(pair.shape, lambda i: (0, 0, 0)) for pair in pairs]
         + [pl.BlockSpec(memory_space=pl.ANY)] * len(earlier)
-        + [in_block] * len(carry),
+        + [row_block] * len(carry),
         out_specs=out_specs,
+        scratch_shapes=[pltpu.VMEM((block, HEAD_DIM), jnp.bfloat16)],
         out_shape=out_shape,
         compiler_params=pltpu.CompilerParams(vmem_limit_bytes=VMEM_LIMIT),
         cost_estimate=pl.CostEstimate(
@@ -223,7 +229,7 @@
             transcendentals=rows * tokens,
         ),
         name="attention",
-    )(query, *pairs, *earlier, *carry)
+    )(*turned, *pairs, *earlier, *carry)
 
 
 def output_kernel(place, *refs, groups, count):
@@ -347,15 +353,14 @@
     with jax.named_scope("out_weight_columns"):
         of_xz = jnp.stack(after(of_xz, projected)).reshape(8, 4, 32, WIDE)
         out_columns = [of_xz, across_cores(of_xz)]
-    query = jnp.concatenate([block[0] for block in turned], axis=0)
     near = jnp.concatenate([block[1:3] for block in turned], axis=1)
     far = across_x(near)
-    carry = attention(query, [near, across_cores(near)], [], False, 0, 1, out_columns)
+    carry = attention(turned, [near, across_cores(near)], [], False, out_columns)
     far = after(far, carry)
     with jax.named_scope("joint_weight"):
         joint_share = after(joint_share, near).reshape(4, 32, WIDE)
         joint_columns = lax.all_gather(joint_share, "seq", axis=0)
-    attended = attention(query, [far, across_cores(far)], carry, True, 0, 1, [early])
+    attended = attention(turned, [far, across_cores(far)], carry, True, [early])
 
     attended = attended.reshape(4, ROWS, HEAD_DIM)
     attended = [attended[0]] + [along_z(attended[by], 4 - by) for by in (1, 2, 3)]

time: 223 us -> 221 us (level)
  local copies, waits for them, and re-layouts: 16.9 us -> 13.4 us
    squeeze x4 -> x0, local copies, waits for them, and re-layouts: 2.88 us -> none  [body(): query = jnp.concatenate([block[0] for block in turned], axis=0)]
    ppermute x3, waiting for transfers between devices: 2.87 us -> 5.68 us  [across_cores(): return lax.ppermute(value, 'seq', seq_pairs(lambda h, z, c: (h, z, 1 - c)))]
    unnamed x38 -> x36, local copies, waits for them, and re-layouts: 6.24 us -> 4.76 us
  transfers between devices with their start and end apart: 30 -> 30, of which waited for: 18 -> 20; matrix products, arithmetic and copies ran while one was open for 7% -> 6% of each run, Pallas kernels for 31% -> 32%
where the time goes in v3:
time: 221 us; the launch traced here: 219 us
  waiting for transfers between devices  79.4 us (36%)
  Pallas kernels  69.4 us (31%)
  starting transfers between devices  35.9 us (16%)
  between operations  13.5 us (6%)
  local copies, waits for them, and re-layouts  13.4 us (6%)
  other arithmetic  7.82 us (4%)
    ppermute x9, waiting for transfers between devices, along_z(): lax.ppermute(value, 'seq', seq_pairs(lambda h, z, c: (h, (z + by) % 4, c)))  39.6 us
    pallas_call x2, Pallas kernels, attention(): pl.pallas_call(functools.partial(attention_kernel, count=len(pairs), gate...  28.5 us
    pallas_call x3, Pallas kernels, output(): pl.pallas_call(functools.partial(output_kernel, groups=len(groups), count...  19.4 us
    ppermute x9, starting transfers between devices, along_z(): lax.ppermute(value, 'seq', seq_pairs(lambda h, z, c: (h, (z + by) % 4, c)))  14.6 us
    ppermute x9, waiting for transfers between devices, along_y(): return lax.ppermute(value, 'tp', [(i, (i + by) % 4) for i in range(4)])  14.1 us
    pallas_call x1, Pallas kernels, qkv(): pl.pallas_call(qkv_kernel, in_specs=[pl.BlockSpec(memory_space=pltpu.SMEM...  13.9 us
    ppermute x9, starting transfers between devices, along_y(): return lax.ppermute(value, 'tp', [(i, (i + by) % 4) for i in range(4)])  12.3 us
    ppermute x2, waiting for transfers between devices, across_x(): return lax.ppermute(value, 'seq', seq_pairs(lambda h, z, c: (1 - h, z, c)))  9.54 us
  transfers between devices with their start and end apart: 30, of which 20 were waited for; matrix products, arithmetic and copies ran while one was open for 6% of the time, Pallas kernels for 32%

profile of v3, /device:TPU:2, one launch (start us, length us, event | category | flops | bytes accessed | tf_op | source)
XLA Modules:
  0.0 219.4 jit_solution(1942029122765012254)
XLA Ops:
  6.5 0.7 all-gather.6.cloned.1.call-update
  7.4 1.2 constant_dynamic-slice_fusion.6
  8.6 1.6 collective-permute-start
  10.2 2.9 %collective-permute-start.1 = (bf16[32,1024]{1,0:T(8,128)(2,1)S(1)}, bf16[32,1024]{1,0:T(8,128)(2,1)S(1)}, u32[]{:S(2)}, u32[]{:S(2)}) collective-permute-start(bf16[32,1024]{1,0:T(8,128)(2,1)S(1)} %get-tuple-element.32), channel_id=1, source_target_pairs={{0,2},{1,3},{2,0},{3,1},{4,6},{5,7},{6,4},{7,5},{8,10},{9,11},{10,... | collective-permute-start | bytes 196616 | tf_op jit(solution)/shard_map/out_weight_columns/ppermute | solution.py:43
  13.1 1.3 collective-permute-start.2
  14.5 0.9 slice.87
  15.4 0.9 collective-permute-done.1
  16.3 1.1 collective-permute-done.2
  17.5 2.2 %collective-permute-start.4 = (bf16[4,32,1024]{2,1,0:T(8,128)(2,1)S(1)}, bf16[4,32,1024]{2,1,0:T(8,128)(2,1)S(1)}, u32[]{:S(2)}, u32[]{:S(2)}) collective-permute-start(bf16[4,32,1024]{2,1,0:T(8,128)(2,1)S(1)} %get-tuple-element.43), channel_id=1, source_target_pairs={{0,32},{4,36},{8,40},{12,44},{16,48},{20,52},{24,56},{28,60},{32,0... | collective-permute-start | bytes 786440 | tf_op jit(solution)/shard_map/out_weight_columns/ppermute | solution.py:35
  20.2 1.3 collective-permute-start.3
  21.5 4.2 %collective-permute-done.4 = bf16[4,32,1024]{2,1,0:T(8,128)(2,1)S(1)} collective-permute-done((bf16[4,32,1024]{2,1,0:T(8,128)(2,1)S(1)}, bf16[4,32,1024]{2,1,0:T(8,128)(2,1)S(1)}, u32[]{:S(2)}, u32[]{:S(2)}) %collective-permute-start.4) | collective-permute-done | bytes 262176 | tf_op jit(solution)/shard_map/out_weight_columns/ppermute | solution.py:35
  25.8 2.0 collective-permute-start.5
  27.8 3.6 %collective-permute-start.6 = (bf16[2,4,32,1024]{3,2,1,0:T(8,128)(2,1)S(1)}, bf16[2,4,32,1024]{3,2,1,0:T(8,128)(2,1)}, u32[]{:S(2)}, u32[]{:S(2)}) collective-permute-start(bf16[2,4,32,1024]{3,2,1,0:T(8,128)(2,1)S(1)} %pad_maximum_fusion.2), channel_id=1, source_target_pairs={{0,16},{4,20},{8,24},{12,28},{16,0},{20,4},{24,8},{28,12},{32,48},... | collective-permute-start | bytes 1572872 | tf_op jit(solution)/shard_map/out_weight_columns/ppermute | solution.py:31
  31.3 1.0 collective-permute-start.7
  32.3 0.8 fusion.1.one
  33.1 3.8 %collective-permute-done.3 = bf16[256,1024]{1,0:T(8,128)(2,1)S(1)} collective-permute-done((bf16[256,1024]{1,0:T(8,128)(2,1)S(1)}, bf16[256,1024]{1,0:T(8,128)(2,1)S(1)}, u32[]{:S(2)}, u32[]{:S(2)}) %collective-permute-start.3) | collective-permute-done | bytes 524320 | tf_op jit(solution)/shard_map/ppermute | solution.py:341
  37.0 0.9 slice_select_fusion.two
  37.9 4.0 %collective-permute-done.5 = bf16[2,4,32,1024]{3,2,1,0:T(8,128)(2,1)S(1)} collective-permute-done((bf16[2,4,32,1024]{3,2,1,0:T(8,128)(2,1)S(1)}, bf16[2,4,32,1024]{3,2,1,0:T(8,128)(2,1)S(1)}, u32[]{:S(2)}, u32[]{:S(2)}) %collective-permute-start.5) | collective-permute-done | bytes 524320 | tf_op jit(solution)/shard_map/out_weight_columns/ppermute | solution.py:31
  41.8 10.2 %collective-permute-done.6 = bf16[2,4,32,1024]{3,2,1,0:T(8,128)(2,1)} collective-permute-done((bf16[2,4,32,1024]{3,2,1,0:T(8,128)(2,1)S(1)}, bf16[2,4,32,1024]{3,2,1,0:T(8,128)(2,1)}, u32[]{:S(2)}, u32[]{:S(2)}) %collective-permute-start.6) | collective-permute-done | bytes 524320 | tf_op jit(solution)/shard_map/out_weight_columns/ppermute | solution.py:31
  52.0 7.6 %products.1 = (bf16[128,4096]{1,0:T(8,128)(2,1)}, bf16[256,4096]{1,0:T(8,128)(2,1)}) custom-call(bf16[128,1024]{1,0:T(8,128)(2,1)} %fusion.1.one, bf16[256,1024]{1,0:T(8,128)(2,1)} %slice_select_fusion.two, bf16[1024,4096]{1,0:T(8,128)(2,1)} %right.1), custom_call_target="tpu_custom_call" | custom-call | flops 3221225472 | bytes 1048576 | tf_op jit(solution)/shard_map/products/pallas_call | solution.py:140
  59.6 0.7 reduce-scatter.3.cloned.1.call-update
  60.6 0.6 stack.97.place
  61.1 13.9 %qkv.1 = bf16[4,3,512,128]{3,2,1,0:T(8,128)(2,1)} custom-call(s32[5]{0:T(128)} %stack.97.place, bf16[512,4096]{1,0:T(8,128)(2,1)} %bitcast.83, f32[4,4096]{1,0:T(4,128)} %bitcast.81, bf16[3,4096,512]{2,1,0:T(8,128)(2,1)} %bitcast.82, bf16[128,4096]{1,0:T(8,128)(2,1)} %get-tuple-element.18.rest_0_, bf16[256,4096]{1,0:T(8,128)(2,1)} %get-tuple-element.19.rest_1_), custom_call_target="tpu_custom_call" | custom-call | flops 6442450944 | bytes 1048576 | tf_op jit(solution)/shard_map/qkv/pallas_call | solution.py:114
  75.0 2.2 slice_bitcast_fusion
  77.2 1.2 collective-permute-start.8
  78.5 2.4 %collective-permute-start.9 = (bf16[3,512,128]{2,1,0:T(8,128)(2,1)S(1)}, bf16[3,512,128]{2,1,0:T(8,128)(2,1)S(1)}, u32[]{:S(2)}, u32[]{:S(2)}) collective-permute-start(bf16[3,512,128]{2,1,0:T(8,128)(2,1)S(1)} %get-tuple-element.34), channel_id=1, source_target_pairs={{0,16},{4,20},{8,24},{12,28},{16,0},{20,4},{24,8},{28,12},{32,48},... | collective-permute-start | bytes 1179656 | tf_op jit(solution)/shard_map/ppermute | solution.py:31
  80.8 1.2 collective-permute-start.10
  82.1 1.0 slice_bitcast_fusion.4
  83.1 5.6 %collective-permute-done.8.refs_1_ = bf16[3,512,128]{2,1,0:T(8,128)(2,1)S(1)} collective-permute-done((bf16[3,512,128]{2,1,0:T(8,128)(2,1)S(1)}, bf16[3,512,128]{2,1,0:T(8,128)(2,1)S(1)}, u32[]{:S(2)}, u32[]{:S(2)}) %collective-permute-start.8) | collective-permute-done | bytes 393248 | tf_op jit(solution)/shard_map/ppermute | solution.py:31
  88.7 9.6 %collective-permute-done.9.refs_2_ = bf16[3,512,128]{2,1,0:T(8,128)(2,1)S(1)} collective-permute-done((bf16[3,512,128]{2,1,0:T(8,128)(2,1)S(1)}, bf16[3,512,128]{2,1,0:T(8,128)(2,1)S(1)}, u32[]{:S(2)}, u32[]{:S(2)}) %collective-permute-start.9) | collective-permute-done | bytes 393248 | tf_op jit(solution)/shard_map/ppermute | solution.py:31
  98.3 1.2 pad_maximum_fusion.1.refs_4_
  99.5 1.5 pad_maximum_fusion
  101.1 0.5 collective-permute-start.12
  101.6 2.1 collective-permute-start.11
  103.8 2.9 %collective-permute-done.12.refs_5_ = bf16[2,2048,128]{2,1,0:T(8,128)(2,1)S(1)} collective-permute-done((bf16[2,2048,128]{2,1,0:T(8,128)(2,1)}, bf16[2,2048,128]{2,1,0:T(8,128)(2,1)S(1)}, u32[]{:S(2)}, u32[]{:S(2)}) %collective-permute-start.12) | collective-permute-done | bytes 1048608 | tf_op jit(solution)/shard_map/ppermute | solution.py:39
  106.8 0.8 copy-done.17
  107.6 1.4 copy-done.5
  109.0 14.2 %attention.2 = (f32[2048,128]{1,0:T(8,128)}, f32[2048,128]{1,0:T(8,128)}, f32[2048,128]{1,0:T(8,128)}) custom-call(bf16[3,512,128]{2,1,0:T(8,128)(2,1)} %get-tuple-element.36.refs_0_, bf16[3,512,128]{2,1,0:T(8,128)(2,1)} %copy-done.12, bf16[3,512,128]{2,1,0:T(8,128)(2,1)} %copy-done.13, bf16[3,512,128]{2,1,0:T(8,128)(2,1)} %copy-done.14, ...), custom_call_target="tpu_custom_call" | custom-call | flops 4294967296 | bytes 2097152 | tf_op jit(solution)/shard_map/attention/pallas_call | solution.py:215
  123.2 5.3 %collective-permute-done.11.refs_4_ = bf16[2,2048,128]{2,1,0:T(8,128)(2,1)S(1)} collective-permute-done((bf16[2,2048,128]{2,1,0:T(8,128)(2,1)}, bf16[2,2048,128]{2,1,0:T(8,128)(2,1)S(1)}, u32[]{:S(2)}, u32[]{:S(2)}) %collective-permute-start.11) | collective-permute-done | bytes 1048608 | tf_op jit(solution)/shard_map/ppermute | solution.py:35
  128.5 2.7 %collective-permute-done.14.refs_5_ = bf16[2,2048,128]{2,1,0:T(8,128)(2,1)S(1)} collective-permute-done((bf16[2,2048,128]{2,1,0:T(8,128)(2,1)S(1)}, bf16[2,2048,128]{2,1,0:T(8,128)(2,1)S(1)}, u32[]{:S(2)}, u32[]{:S(2)}) %collective-permute-start.14) | collective-permute-done | bytes 1048608 | tf_op jit(solution)/shard_map/ppermute | solution.py:39
  131.2 1.0 copy-done.16
  132.2 14.3 %attention.3 = bf16[2048,128]{1,0:T(8,128)(2,1)} custom-call(bf16[3,512,128]{2,1,0:T(8,128)(2,1)} %get-tuple-element.36.refs_0_, bf16[3,512,128]{2,1,0:T(8,128)(2,1)} %copy-done.12, bf16[3,512,128]{2,1,0:T(8,128)(2,1)} %copy-done.13, bf16[3,512,128]{2,1,0:T(8,128)(2,1)} %copy-done.14, bf16[2,2048,128]{2,1,0:T(8,128)(2,1)} %copy-done.15, ...), custom_call_target="tpu_custom_call" | custom-call | flops 4294967296 | bytes 2097152 | tf_op jit(solution)/shard_map/attention/pallas_call | solution.py:215
  146.5 1.1 fusion.3
  147.5 2.0 collective-permute-start.15
  149.5 1.1 collective-permute-start.16
  150.7 0.9 slice_bitcast_fusion.8
  151.5 4.6 %collective-permute-done.15 = bf16[512,128]{1,0:T(8,128)(2,1)S(1)} collective-permute-done((bf16[512,128]{1,0:T(8,128)(2,1)S(1)}, bf16[512,128]{1,0:T(8,128)(2,1)S(1)}, u32[]{:S(2)}, u32[]{:S(2)}) %collective-permute-start.15) | collective-permute-done | bytes 131104 | tf_op jit(solution)/shard_map/ppermute | solution.py:31
  156.2 2.9 %collective-permute-done.16 = bf16[512,128]{1,0:T(8,128)(2,1)S(1)} collective-permute-done((bf16[512,128]{1,0:T(8,128)(2,1)S(1)}, bf16[512,128]{1,0:T(8,128)(2,1)S(1)}, u32[]{:S(2)}, u32[]{:S(2)}) %collective-permute-start.16) | collective-permute-done | bytes 131104 | tf_op jit(solution)/shard_map/ppermute | solution.py:31
  159.1 2.8 %collective-permute-done.17 = bf16[512,128]{1,0:T(8,128)(2,1)S(1)} collective-permute-done((bf16[512,128]{1,0:T(8,128)(2,1)S(1)}, bf16[512,128]{1,0:T(8,128)(2,1)S(1)}, u32[]{:S(2)}, u32[]{:S(2)}) %collective-permute-start.17) | collective-permute-done | bytes 131104 | tf_op jit(solution)/shard_map/ppermute | solution.py:31
  162.0 3.0 %collective-permute-start.19 = (bf16[4,256,128]{2,1,0:T(8,128)(2,1)S(1)}, bf16[4,256,128]{2,1,0:T(8,128)(2,1)S(1)}, u32[]{:S(2)}, u32[]{:S(2)}) collective-permute-start(bf16[4,256,128]{2,1,0:T(8,128)(2,1)S(1)} %pad_maximum_fusion.5.refs_0_), channel_id=1, source_target_pairs={{0,2},{1,3},{2,0},{3,1},{4,6},{5,7},{6,4},{7,5},{8,10},{9,11},{10,... | collective-permute-start | bytes 786440 | tf_op jit(solution)/shard_map/ppermute | solution.py:43
  165.5 1.7 collective-permute-start.21
  167.2 1.2 collective-permute-start.22
  168.4 9.6 %collective-permute-done.18.refs_1_ = bf16[4,256,128]{2,1,0:T(8,128)(2,1)S(1)} collective-permute-done((bf16[4,256,128]{2,1,0:T(8,128)(2,1)S(1)}, bf16[4,256,128]{2,1,0:T(8,128)(2,1)S(1)}, u32[]{:S(2)}, u32[]{:S(2)}) %collective-permute-start.18) | collective-permute-done | bytes 262176 | tf_op jit(solution)/shard_map/ppermute | solution.py:43
  178.0 0.6 dynamic-slice_bitcast_fusion.3.refs_10_.refs_5_
  179.6 5.6 %residual.2 = bf16[256,1024]{1,0:T(8,128)(2,1)} custom-call(s32[5]{0:T(128)} %stack.97.place, bf16[4,256,128]{2,1,0:T(8,128)(2,1)} %copy-done.3, bf16[4,256,128]{2,1,0:T(8,128)(2,1)} %copy-done.6, bf16[4,256,128]{2,1,0:T(8,128)(2,1)} %copy-done.7, bf16[4,256,128]{2,1,0:T(8,128)(2,1)} %copy-done.8, ...), custom_call_target="tpu_custom_call" | custom-call | flops 1073741824 | bytes 1048576 | tf_op jit(solution)/shard_map/residual/pallas_call | solution.py:289
  185.3 1.3 collective-permute-start.24
  186.6 1.6 collective-permute-done.21.refs_5_.refs_1_
  188.2 0.7 collective-permute-done.23.refs_7_.refs_3_
  189.0 0.7 copy-done.11
  189.7 5.4 %residual.3 = bf16[256,1024]{1,0:T(8,128)(2,1)} custom-call(s32[5]{0:T(128)} %stack.97.place, bf16[4,256,128]{2,1,0:T(8,128)(2,1)} %copy-done.4, bf16[4,256,128]{2,1,0:T(8,128)(2,1)} %copy-done.9, bf16[4,256,128]{2,1,0:T(8,128)(2,1)} %copy-done.10, bf16[4,256,128]{2,1,0:T(8,128)(2,1)} %copy-done.11, ...), custom_call_target="tpu_custom_call" | custom-call | flops 1073741824 | bytes 1048576 | tf_op jit(solution)/shard_map/residual/pallas_call | solution.py:289
  195.1 1.3 collective-permute-start.25
  196.4 8.3 %blended.1 = f32[512,1024]{1,0:T(8,128)} custom-call(s32[5]{0:T(128)} %stack.97.place, bf16[4,256,128]{2,1,0:T(8,128)(2,1)} %copy-done.3, bf16[4,256,128]{2,1,0:T(8,128)(2,1)} %copy-done.6, bf16[4,256,128]{2,1,0:T(8,128)(2,1)} %copy-done.7, bf16[4,256,128]{2,1,0:T(8,128)(2,1)} %copy-done.8, bf16[4,256,128]{2,1,0:T(8,128)(2,1)} %copy-done.4, ...), custom_call_target="tpu_custom_call" | custom-call | flops 2147483648 | bytes 1048576 | tf_op jit(solution)/shard_map/blended/pallas_call | solution.py:289
  204.8 5.2 %collective-permute-done.25 = bf16[256,1024]{1,0:T(8,128)(2,1)S(1)} collective-permute-done((bf16[256,1024]{1,0:T(8,128)(2,1)}, bf16[256,1024]{1,0:T(8,128)(2,1)S(1)}, u32[]{:S(2)}, u32[]{:S(2)}) %collective-permute-start.25) | collective-permute-done | bytes 524320 | tf_op jit(solution)/shard_map/ppermute | solution.py:375
  210.0 2.9 %fusion = bf16[1,512,1024]{2,1,0:T(8,128)(2,1)} fusion(f32[512,1024]{1,0:T(8,128)} %blended.1, bf16[256,1024]{1,0:T(8,128)(2,1)S(1)} %collective-permute-done.25, bf16[256,1024]{1,0:T(8,128)(2,1)S(1)} %collective-permute-done.24), kind=kLoop, calls=%fused_computation.3 | loop fusion | flops 3145728 | bytes 4194304 | tf_op jit(solution)/shard_map/broadcast_in_dim | solution.py:379
  (71 shorter events, 3.1 us)
Async XLA Ops:
  6.5 13.2 %copy-start = (bf16[1,512,1024]{2,1,0:T(8,128)(2,1)S(1)}, bf16[1,512,1024]{2,1,0:T(8,128)(2,1)}, u32[]{:S(2)}) copy-start(bf16[1,512,1024]{2,1,0:T(8,128)(2,1)} %param.6) | copy-start | bytes 3145732
  6.5 13.2 %copy-start.2 = (bf16[1,512,1024]{2,1,0:T(8,128)(2,1)S(1)}, bf16[1,512,1024]{2,1,0:T(8,128)(2,1)}, u32[]{:S(2)}) copy-start(bf16[1,512,1024]{2,1,0:T(8,128)(2,1)} %param.11) | copy-start | bytes 3145732
  6.5 54.6 %all-gather.6.cloned.1.call-start = ((), (), s32[]{:S(2)}) async-start(), calls=%async_computation.5 | async-start | bytes 5242880 | tf_op jit(solution)/shard_map/all_gather | solution.py:329
  7.3 92.2 %reduce-scatter.5.cloned.1.call-start = ((), (), s32[]{:S(2)}) async-start(), calls=%async_computation.3 | async-start | bytes 1310720 | tf_op jit(solution)/shard_map/reduce_scatter | solution.py:345
  8.6 6.9 %collective-permute-start = (bf16[32,1024]{1,0:T(8,128)(2,1)S(1)}, bf16[32,1024]{1,0:T(8,128)(2,1)S(1)}, u32[]{:S(2)}, u32[]{:S(2)}) collective-permute-start(bf16[32,1024]{1,0:T(8,128)(2,1)S(1)} %get-tuple-element.30), channel_id=1, source_target_pairs={{0,1},{1,2},{2,3},{3,0},{4,5},{5,6},{6,7},{7,4},{8,9},{9,10},{10,1... | collective-permute-start | bytes 196616 | tf_op jit(solution)/shard_map/out_weight_columns/ppermute | solution.py:43
  10.2 6.1 %collective-permute-start.1 = (bf16[32,1024]{1,0:T(8,128)(2,1)S(1)}, bf16[32,1024]{1,0:T(8,128)(2,1)S(1)}, u32[]{:S(2)}, u32[]{:S(2)}) collective-permute-start(bf16[32,1024]{1,0:T(8,128)(2,1)S(1)} %get-tuple-element.32), channel_id=1, source_target_pairs={{0,2},{1,3},{2,0},{3,1},{4,6},{5,7},{6,4},{7,5},{8,10},{9,11},{10,... | collective-permute-start | bytes 196616 | tf_op jit(solution)/shard_map/out_weight_columns/ppermute | solution.py:43
  13.1 4.3 %collective-permute-start.2 = (bf16[32,1024]{1,0:T(8,128)(2,1)S(1)}, bf16[32,1024]{1,0:T(8,128)(2,1)S(1)}, u32[]{:S(2)}, u32[]{:S(2)}) collective-permute-start(bf16[32,1024]{1,0:T(8,128)(2,1)S(1)} %get-tuple-element.31), channel_id=1, source_target_pairs={{0,3},{1,0},{2,1},{3,2},{4,7},{5,4},{6,5},{7,6},{8,11},{9,8},{10,9... | collective-permute-start | bytes 196616 | tf_op jit(solution)/shard_map/out_weight_columns/ppermute | solution.py:43
  17.5 8.2 %collective-permute-start.4 = (bf16[4,32,1024]{2,1,0:T(8,128)(2,1)S(1)}, bf16[4,32,1024]{2,1,0:T(8,128)(2,1)S(1)}, u32[]{:S(2)}, u32[]{:S(2)}) collective-permute-start(bf16[4,32,1024]{2,1,0:T(8,128)(2,1)S(1)} %get-tuple-element.43), channel_id=1, source_target_pairs={{0,32},{4,36},{8,40},{12,44},{16,48},{20,52},{24,56},{28,60},{32,0... | collective-permute-start | bytes 786440 | tf_op jit(solution)/shard_map/out_weight_columns/ppermute | solution.py:35
  20.2 16.8 %collective-permute-start.3 = (bf16[256,1024]{1,0:T(8,128)(2,1)S(1)}, bf16[256,1024]{1,0:T(8,128)(2,1)S(1)}, u32[]{:S(2)}, u32[]{:S(2)}) collective-permute-start(bf16[256,1024]{1,0:T(8,128)(2,1)S(1)} %slice.113), channel_id=1, source_target_pairs={{0,64},{1,65},{2,66},{3,67},{4,68},{5,69},{6,70},{7,71},{8,72},{9,... | collective-permute-start | bytes 1572872 | tf_op jit(solution)/shard_map/ppermute | solution.py:341
  25.8 16.0 %collective-permute-start.5 = (bf16[2,4,32,1024]{3,2,1,0:T(8,128)(2,1)S(1)}, bf16[2,4,32,1024]{3,2,1,0:T(8,128)(2,1)S(1)}, u32[]{:S(2)}, u32[]{:S(2)}) collective-permute-start(bf16[2,4,32,1024]{3,2,1,0:T(8,128)(2,1)S(1)} %pad_maximum_fusion.2), channel_id=1, source_target_pairs={{0,8},{4,12},{8,16},{12,20},{16,24},{20,28},{24,0},{28,4},{32,40},... | collective-permute-start | bytes 1572872 | tf_op jit(solution)/shard_map/out_weight_columns/ppermute | solution.py:31
  27.8 24.2 %collective-permute-start.6 = (bf16[2,4,32,1024]{3,2,1,0:T(8,128)(2,1)S(1)}, bf16[2,4,32,1024]{3,2,1,0:T(8,128)(2,1)}, u32[]{:S(2)}, u32[]{:S(2)}) collective-permute-start(bf16[2,4,32,1024]{3,2,1,0:T(8,128)(2,1)S(1)} %pad_maximum_fusion.2), channel_id=1, source_target_pairs={{0,16},{4,20},{8,24},{12,28},{16,0},{20,4},{24,8},{28,12},{32,48},... | collective-permute-start | bytes 1572872 | tf_op jit(solution)/shard_map/out_weight_columns/ppermute | solution.py:31
  31.3 20.6 %collective-permute-start.7 = (bf16[2,4,32,1024]{3,2,1,0:T(8,128)(2,1)S(1)}, bf16[2,4,32,1024]{3,2,1,0:T(8,128)(2,1)}, u32[]{:S(2)}, u32[]{:S(2)}) collective-permute-start(bf16[2,4,32,1024]{3,2,1,0:T(8,128)(2,1)S(1)} %pad_maximum_fusion.2), channel_id=1, source_target_pairs={{0,24},{4,28},{8,0},{12,4},{16,8},{20,12},{24,16},{28,20},{32,56},... | collective-permute-start | bytes 1572872 | tf_op jit(solution)/shard_map/out_weight_columns/ppermute | solution.py:31
  59.6 69.0 %reduce-scatter.3.cloned.1.call-start = ((), (), s32[]{:S(2)}) async-start(), calls=%async_computation.2 | async-start | bytes 2621440 | tf_op jit(solution)/shard_map/early_residual/reduce_scatter | solution.py:349
  60.3 118.6 %all-gather.4.cloned.1.call-start = ((), (), s32[]{:S(2)}) async-start(), calls=%async_computation.4 | async-start | bytes 4456448 | tf_op jit(solution)/shard_map/joint_weight/all_gather | solution.py:362
  77.2 11.4 %collective-permute-start.8 = (bf16[3,512,128]{2,1,0:T(8,128)(2,1)S(1)}, bf16[3,512,128]{2,1,0:T(8,128)(2,1)S(1)}, u32[]{:S(2)}, u32[]{:S(2)}) collective-permute-start(bf16[3,512,128]{2,1,0:T(8,128)(2,1)S(1)} %get-tuple-element.35), channel_id=1, source_target_pairs={{0,8},{4,12},{8,16},{12,20},{16,24},{20,28},{24,0},{28,4},{32,40},... | collective-permute-start | bytes 1179656 | tf_op jit(solution)/shard_map/ppermute | solution.py:31
  78.5 19.8 %collective-permute-start.9 = (bf16[3,512,128]{2,1,0:T(8,128)(2,1)S(1)}, bf16[3,512,128]{2,1,0:T(8,128)(2,1)S(1)}, u32[]{:S(2)}, u32[]{:S(2)}) collective-permute-start(bf16[3,512,128]{2,1,0:T(8,128)(2,1)S(1)} %get-tuple-element.34), channel_id=1, source_target_pairs={{0,16},{4,20},{8,24},{12,28},{16,0},{20,4},{24,8},{28,12},{32,48},... | collective-permute-start | bytes 1179656 | tf_op jit(solution)/shard_map/ppermute | solution.py:31
  80.8 17.5 %collective-permute-start.10 = (bf16[3,512,128]{2,1,0:T(8,128)(2,1)S(1)}, bf16[3,512,128]{2,1,0:T(8,128)(2,1)S(1)}, u32[]{:S(2)}, u32[]{:S(2)}) collective-permute-start(bf16[3,512,128]{2,1,0:T(8,128)(2,1)S(1)} %get-tuple-element.33), channel_id=1, source_target_pairs={{0,24},{4,28},{8,0},{12,4},{16,8},{20,12},{24,16},{28,20},{32,56},... | collective-permute-start | bytes 1179656 | tf_op jit(solution)/shard_map/ppermute | solution.py:31
  88.7 12.3 %copy-start.12 = (bf16[3,512,128]{2,1,0:T(8,128)(2,1)}, bf16[3,512,128]{2,1,0:T(8,128)(2,1)S(1)}, u32[]{:S(2)}) copy-start(bf16[3,512,128]{2,1,0:T(8,128)(2,1)S(1)} %collective-permute-done.8.refs_1_) | copy-start | bytes 1179652
  98.3 2.7 %copy-start.13 = (bf16[3,512,128]{2,1,0:T(8,128)(2,1)}, bf16[3,512,128]{2,1,0:T(8,128)(2,1)S(1)}, u32[]{:S(2)}) copy-start(bf16[3,512,128]{2,1,0:T(8,128)(2,1)S(1)} %collective-permute-done.9.refs_2_) | copy-start | bytes 1179652
  98.3 2.7 %copy-start.14 = (bf16[3,512,128]{2,1,0:T(8,128)(2,1)}, bf16[3,512,128]{2,1,0:T(8,128)(2,1)S(1)}, u32[]{:S(2)}) copy-start(bf16[3,512,128]{2,1,0:T(8,128)(2,1)S(1)} %collective-permute-done.10.refs_3_) | copy-start | bytes 1179652
  101.0 6.6 %copy-start.1 = (bf16[4,2,4,32,1024]{4,3,2,1,0:T(8,128)(2,1)}, bf16[4,2,4,32,1024]{4,3,2,1,0:T(8,128)(2,1)S(1)}, u32[]{:S(2)}) copy-start(bf16[4,2,4,32,1024]{4,3,2,1,0:T(8,128)(2,1)S(1)} %pad_maximum_fusion) | copy-start | bytes 6291460
  101.0 5.7 %collective-permute-start.13 = (bf16[8,4,32,1024]{3,2,1,0:T(8,128)(2,1)S(1)}, bf16[8,4,32,1024]{3,2,1,0:T(8,128)(2,1)S(1)}, u32[]{:S(2)}, u32[]{:S(2)}) collective-permute-start(bf16[8,4,32,1024]{3,2,1,0:T(8,128)(2,1)S(1)} %bitcast.68), channel_id=1, source_target_pairs={{0,4},{4,0},{8,12},{12,8},{16,20},{20,16},{24,28},{28,24},{32,36},... | collective-permute-start | bytes 6291464 | tf_op jit(solution)/shard_map/out_weight_columns/ppermute | solution.py:39
  101.1 5.5 %collective-permute-start.12 = (bf16[2,2048,128]{2,1,0:T(8,128)(2,1)}, bf16[2,2048,128]{2,1,0:T(8,128)(2,1)S(1)}, u32[]{:S(2)}, u32[]{:S(2)}) collective-permute-start(bf16[2,2048,128]{2,1,0:T(8,128)(2,1)} %pad_maximum_fusion.1.refs_4_), channel_id=1, source_target_pairs={{0,4},{4,0},{8,12},{12,8},{16,20},{20,16},{24,28},{28,24},{32,36},... | collective-permute-start | bytes 3145736 | tf_op jit(solution)/shard_map/ppermute | solution.py:39
  101.6 26.9 %collective-permute-start.11 = (bf16[2,2048,128]{2,1,0:T(8,128)(2,1)}, bf16[2,2048,128]{2,1,0:T(8,128)(2,1)S(1)}, u32[]{:S(2)}, u32[]{:S(2)}) collective-permute-start(bf16[2,2048,128]{2,1,0:T(8,128)(2,1)} %pad_maximum_fusion.1.refs_4_), channel_id=1, source_target_pairs={{0,32},{4,36},{8,40},{12,44},{16,48},{20,52},{24,56},{28,60},{32,0... | collective-permute-start | bytes 3145736 | tf_op jit(solution)/shard_map/ppermute | solution.py:35
  106.6 1.0 copy-start.17
  107.6 1.4 copy-start.5
  128.5 2.7 %copy-start.15 = (bf16[2,2048,128]{2,1,0:T(8,128)(2,1)}, bf16[2,2048,128]{2,1,0:T(8,128)(2,1)S(1)}, u32[]{:S(2)}) copy-start(bf16[2,2048,128]{2,1,0:T(8,128)(2,1)S(1)} %collective-permute-done.11.refs_4_) | copy-start | bytes 3145732
  128.5 2.7 %collective-permute-start.14 = (bf16[2,2048,128]{2,1,0:T(8,128)(2,1)S(1)}, bf16[2,2048,128]{2,1,0:T(8,128)(2,1)S(1)}, u32[]{:S(2)}, u32[]{:S(2)}) collective-permute-start(bf16[2,2048,128]{2,1,0:T(8,128)(2,1)S(1)} %collective-permute-done.11.refs_4_), channel_id=1, source_target_pairs={{0,4},{4,0},{8,12},{12,8},{16,20},{20,16},{24,28},{28,24},{32,36},... | collective-permute-start | bytes 3145736 | tf_op jit(solution)/shard_map/ppermute | solution.py:39
  131.2 1.0 copy-start.16
  147.5 8.7 %collective-permute-start.15 = (bf16[512,128]{1,0:T(8,128)(2,1)S(1)}, bf16[512,128]{1,0:T(8,128)(2,1)S(1)}, u32[]{:S(2)}, u32[]{:S(2)}) collective-permute-start(bf16[512,128]{1,0:T(8,128)(2,1)S(1)} %get-tuple-element.39), channel_id=1, source_target_pairs={{0,24},{4,28},{8,0},{12,4},{16,8},{20,12},{24,16},{28,20},{32,56},... | collective-permute-start | bytes 393224 | tf_op jit(solution)/shard_map/ppermute | solution.py:31
  149.5 9.5 %collective-permute-start.16 = (bf16[512,128]{1,0:T(8,128)(2,1)S(1)}, bf16[512,128]{1,0:T(8,128)(2,1)S(1)}, u32[]{:S(2)}, u32[]{:S(2)}) collective-permute-start(bf16[512,128]{1,0:T(8,128)(2,1)S(1)} %get-tuple-element.41), channel_id=1, source_target_pairs={{0,16},{4,20},{8,24},{12,28},{16,0},{20,4},{24,8},{28,12},{32,48},... | collective-permute-start | bytes 393224 | tf_op jit(solution)/shard_map/ppermute | solution.py:31
  150.6 11.2 %collective-permute-start.17 = (bf16[512,128]{1,0:T(8,128)(2,1)S(1)}, bf16[512,128]{1,0:T(8,128)(2,1)S(1)}, u32[]{:S(2)}, u32[]{:S(2)}) collective-permute-start(bf16[512,128]{1,0:T(8,128)(2,1)S(1)} %get-tuple-element.40), channel_id=1, source_target_pairs={{0,8},{4,12},{8,16},{12,20},{16,24},{20,28},{24,0},{28,4},{32,40},... | collective-permute-start | bytes 393224 | tf_op jit(solution)/shard_map/ppermute | solution.py:31
  161.9 17.0 %copy-start.3 = (bf16[4,256,128]{2,1,0:T(8,128)(2,1)}, bf16[4,256,128]{2,1,0:T(8,128)(2,1)S(1)}, u32[]{:S(2)}) copy-start(bf16[4,256,128]{2,1,0:T(8,128)(2,1)S(1)} %pad_maximum_fusion.5.refs_0_) | copy-start | bytes 786436
  161.9 16.1 %collective-permute-start.18 = (bf16[4,256,128]{2,1,0:T(8,128)(2,1)S(1)}, bf16[4,256,128]{2,1,0:T(8,128)(2,1)S(1)}, u32[]{:S(2)}, u32[]{:S(2)}) collective-permute-start(bf16[4,256,128]{2,1,0:T(8,128)(2,1)S(1)} %pad_maximum_fusion.5.refs_0_), channel_id=1, source_target_pairs={{0,1},{1,2},{2,3},{3,0},{4,5},{5,6},{6,7},{7,4},{8,9},{9,10},{10,1... | collective-permute-start | bytes 786440 | tf_op jit(solution)/shard_map/ppermute | solution.py:43
  162.0 16.6 %collective-permute-start.19 = (bf16[4,256,128]{2,1,0:T(8,128)(2,1)S(1)}, bf16[4,256,128]{2,1,0:T(8,128)(2,1)S(1)}, u32[]{:S(2)}, u32[]{:S(2)}) collective-permute-start(bf16[4,256,128]{2,1,0:T(8,128)(2,1)S(1)} %pad_maximum_fusion.5.refs_0_), channel_id=1, source_target_pairs={{0,2},{1,3},{2,0},{3,1},{4,6},{5,7},{6,4},{7,5},{8,10},{9,11},{10,... | collective-permute-start | bytes 786440 | tf_op jit(solution)/shard_map/ppermute | solution.py:43
  165.0 13.9 %collective-permute-start.20 = (bf16[4,256,128]{2,1,0:T(8,128)(2,1)S(1)}, bf16[4,256,128]{2,1,0:T(8,128)(2,1)S(1)}, u32[]{:S(2)}, u32[]{:S(2)}) collective-permute-start(bf16[4,256,128]{2,1,0:T(8,128)(2,1)S(1)} %pad_maximum_fusion.5.refs_0_), channel_id=1, source_target_pairs={{0,3},{1,0},{2,1},{3,2},{4,7},{5,4},{6,5},{7,6},{8,11},{9,8},{10,9... | collective-permute-start | bytes 786440 | tf_op jit(solution)/shard_map/ppermute | solution.py:43
  165.5 19.8 %copy-start.4 = (bf16[4,256,128]{2,1,0:T(8,128)(2,1)}, bf16[4,256,128]{2,1,0:T(8,128)(2,1)S(1)}, u32[]{:S(2)}) copy-start(bf16[4,256,128]{2,1,0:T(8,128)(2,1)S(1)} %pad_maximum_fusion.6.refs_4_.refs_0_) | copy-start | bytes 786436
  165.5 22.6 %collective-permute-start.21 = (bf16[4,256,128]{2,1,0:T(8,128)(2,1)S(1)}, bf16[4,256,128]{2,1,0:T(8,128)(2,1)S(1)}, u32[]{:S(2)}, u32[]{:S(2)}) collective-permute-start(bf16[4,256,128]{2,1,0:T(8,128)(2,1)S(1)} %pad_maximum_fusion.6.refs_4_.refs_0_), channel_id=1, source_target_pairs={{0,1},{1,2},{2,3},{3,0},{4,5},{5,6},{6,7},{7,4},{8,9},{9,10},{10,1... | collective-permute-start | bytes 786440 | tf_op jit(solution)/shard_map/ppermute | solution.py:43
  167.2 21.0 %collective-permute-start.22 = (bf16[4,256,128]{2,1,0:T(8,128)(2,1)S(1)}, bf16[4,256,128]{2,1,0:T(8,128)(2,1)S(1)}, u32[]{:S(2)}, u32[]{:S(2)}) collective-permute-start(bf16[4,256,128]{2,1,0:T(8,128)(2,1)S(1)} %pad_maximum_fusion.6.refs_4_.refs_0_), channel_id=1, source_target_pairs={{0,2},{1,3},{2,0},{3,1},{4,6},{5,7},{6,4},{7,5},{8,10},{9,11},{10,... | collective-permute-start | bytes 786440 | tf_op jit(solution)/shard_map/ppermute | solution.py:43
  178.0 0.9 copy-start.6
  178.0 10.8 %collective-permute-start.23 = (bf16[4,256,128]{2,1,0:T(8,128)(2,1)S(1)}, bf16[4,256,128]{2,1,0:T(8,128)(2,1)S(1)}, u32[]{:S(2)}, u32[]{:S(2)}) collective-permute-start(bf16[4,256,128]{2,1,0:T(8,128)(2,1)S(1)} %pad_maximum_fusion.6.refs_4_.refs_0_), channel_id=1, source_target_pairs={{0,3},{1,0},{2,1},{3,2},{4,7},{5,4},{6,5},{7,6},{8,11},{9,8},{10,9... | collective-permute-start | bytes 786440 | tf_op jit(solution)/shard_map/ppermute | solution.py:43
  178.6 0.7 copy-start.7
  178.9 0.7 copy-start.8
  185.3 19.5 %collective-permute-start.24 = (bf16[256,1024]{1,0:T(8,128)(2,1)}, bf16[256,1024]{1,0:T(8,128)(2,1)S(1)}, u32[]{:S(2)}, u32[]{:S(2)}) collective-permute-start(bf16[256,1024]{1,0:T(8,128)(2,1)} %residual.2), channel_id=1, source_target_pairs={{0,64},{1,65},{2,66},{3,67},{4,68},{5,69},{6,70},{7,71},{8,72},{9,... | collective-permute-start | bytes 1572872 | tf_op jit(solution)/shard_map/ppermute | solution.py:375
  188.2 0.7 copy-start.9
  188.2 0.8 copy-start.10
  188.9 0.7 copy-start.11
  195.1 14.8 %collective-permute-start.25 = (bf16[256,1024]{1,0:T(8,128)(2,1)}, bf16[256,1024]{1,0:T(8,128)(2,1)S(1)}, u32[]{:S(2)}, u32[]{:S(2)}) collective-permute-start(bf16[256,1024]{1,0:T(8,128)(2,1)} %residual.3), channel_id=1, source_target_pairs={{0,64},{1,65},{2,66},{3,67},{4,68},{5,69},{6,70},{7,71},{8,72},{9,... | collective-permute-start | bytes 1572872 | tf_op jit(solution)/shard_map/ppermute | solution.py:375
Sparse Core Ops, SparseCore 0:
  9.0 50.6 all-gather.5
  62.1 23.8 reduce-scatter.4
  88.5 29.4 reduce-scatter.2
  120.3 54.2 all-gather.3
